TPU v7x, 512 devices: a whole 4x8x8 slice. The times are simulated.
512 devices in a mesh: traj: 8 (over y), blk: 64 (over z, x, core).
Axes of the slice: x: 4, y: 8, z: 8, core: 2. Of those that a mesh axis runs over, the one named last changes fastest.
Arguments:
- codes: bfloat16 [8, 16384, 512], P('traj', 'blk'), may hold values from -127 to 127, as said below
- row_scale: float32 [8, 16384], P('traj', 'blk'), may hold values from 0.1 to 1
- valid: int32 [8], P('traj'), may hold values from 8192 to 16384, as said below
Outputs:
- whitened: bfloat16 [8, 16384, 512], P('traj', 'blk')
- koopman: float32 [512, 512], replicated
Inputs may be any that keep to these rules, and one draw needn't show every extreme that they name: `codes`: integer levels. One trajectory has all 16384 frames valid.
All inputs are finite; a program needn't handle non-finite values.
Results may differ from a plain program's by a relative error of at most 0.004.
The roundings to bfloat16 on the way count: a program that leaves them out, or rounds other values in their place, can miss the bound.
Values may be sent and summed in bfloat16 or wider, within the bound.
A program may use at most 64 MiB of HBM per device.

v0:
```python
import jax
import jax.numpy as jnp
from jax import lax
from jax.sharding import PartitionSpec as P


def passed_along(shard, axis, by):
    size = lax.axis_size(axis)
    pairs = [(i, i + by) for i in range(size) if 0 <= i + by < size]
    return lax.ppermute(shard, axis, pairs)


def gram_matrix(left_rows, right_rows):
    return lax.dot_general(
        left_rows, right_rows, (((0,), (0,)), ((), ())), preferred_element_type=jnp.float32
    )


def on_device(codes, row_scale, valid):
    frames = codes.shape[1]
    width = codes.shape[2]
    lag_span = frames // 4
    highest = lax.Precision.HIGHEST
    dequant = (codes[0].astype(jnp.float32) * row_scale[0][:, None]).astype(jnp.bfloat16)
    incoming = passed_along(dequant[:lag_span], "blk", -1)
    shifted = jnp.concatenate([dequant[lag_span:], incoming], axis=0)
    position = lax.axis_index("blk") * frames + jnp.arange(frames, dtype=jnp.int32)
    paired = position + lag_span < valid[0]
    lead_rows = jnp.where(paired[:, None], dequant, jnp.zeros_like(dequant))
    trail_rows = jnp.where(paired[:, None], shifted, jnp.zeros_like(shifted))
    instant = gram_matrix(lead_rows, lead_rows) + gram_matrix(trail_rows, trail_rows)
    crossed = gram_matrix(lead_rows, trail_rows)
    totals = jnp.sum(lead_rows, axis=0, dtype=jnp.float32) + jnp.sum(
        trail_rows, axis=0, dtype=jnp.float32
    )
    samples = 2.0 * jnp.sum(paired.astype(jnp.float32))
    samples, totals, instant, crossed = lax.psum(
        (samples, totals, instant, crossed), ("traj", "blk")
    )
    lagged_sum = crossed + crossed.T
    average = totals / samples
    outer_mean = jnp.outer(average, average)
    instant_cov = instant / samples - outer_mean
    lagged_cov = lagged_sum / samples - outer_mean
    factor = jnp.linalg.cholesky(instant_cov)
    whitener = jax.scipy.linalg.solve_triangular(
        factor, jnp.eye(width, dtype=jnp.float32), lower=True
    )
    koopman = jnp.dot(
        jnp.dot(whitener, lagged_cov, precision=highest, preferred_element_type=jnp.float32),
        whitener.T,
        precision=highest,
        preferred_element_type=jnp.float32,
    )
    centered = dequant.astype(jnp.float32) - average[None, :]
    projected = lax.dot_general(
        centered,
        whitener,
        (((1,), (1,)), ((), ())),
        precision=highest,
        preferred_element_type=jnp.float32,
    )
    return (projected.astype(jnp.bfloat16)[None], koopman)


def solution(mesh):
    return jax.shard_map(
        on_device,
        mesh=mesh,
        in_specs=(P("traj", "blk", None), P("traj", "blk"), P("traj")),
        out_specs=(P("traj", "blk", None), P()),
        check_vma=False,
    )
```

profile of v0, /device:TPU:1, one launch (start us, length us, event | category | flops | bytes accessed | tf_op | source)
XLA Modules:
  0.0 464.5 jit_solution(15866225960702754525)
XLA Ops:
  9.0 8.8 %collective-permute-start = (bf16[64,512]{1,0:T(8,128)(2,1)S(1)}, bf16[64,512]{1,0:T(8,128)(2,1)S(1)}, u32[]{:S(2)}, u32[]{:S(2)}) collective-permute-start(bf16[64,512]{1,0:T(8,128)(2,1)S(1)} %slice.134), channel_id=1, source_target_pairs={{1,0},{2,1},{3,2},{4,3},{5,4},{6,5},{7,6},{8,7},{9,8},{10,9},{11,1... | collective-permute-start | bytes 196616 | tf_op jit(solution)/shard_map/ppermute | solution.py:10
  19.6 1.4 fusion.41
  21.0 1.4 convolution_add_fusion
  25.2 103.0 %all-reduce.1 = (f32[512]{0:T(512)S(1)}, f32[]{:T(128)}) all-reduce(f32[512]{0:T(512)S(1)} %add.82, f32[]{:T(128)S(6)} %mul_shard_map.3), channel_id=1, replica_groups=mesh['traj'=8,'blk'=64] {'traj','blk'}, use_global_device_ids=true, to_apply=%region_2.3 | all-reduce | flops 513 | bytes 4104 | tf_op jit(solution)/shard_map/psum | solution.py:37
  128.8 176.1 %all-reduce.5.cloned.1.call-done = (f32[512,512]{0,1:T(8,128)}, f32[512,512]{1,0:T(8,128)}) async-done(((f32[512,512]{0,1:T(8,128)}, f32[512,512]{1,0:T(8,128)}), (f32[512,512]{0,1:T(8,128)}, f32[512,512]{1,0:T(8,128)})) %all-reduce.5.cloned.1.call-update) | async-done | bytes 2097168 | tf_op jit(solution)/shard_map/psum | solution.py:37
  304.9 1.9 multiply_subtract_fusion.1
  309.9 11.7 %cholesky.104 = f32[128,128]{1,0:T(8,128)S(1)} custom-call(f32[128,128]{1,0:T(8,128)S(1)} %cholesky.266), custom_call_target="Cholesky" | custom-call | tf_op jit(solution)/shard_map/jit(cholesky)/cholesky | solution.py:45
  321.8 9.8 %custom-call.31 = f32[1,128,128]{1,2,0:T(8,128)S(1)} custom-call(f32[1,128,128]{2,1,0:T(8,128)S(1)} %get-tuple-element.37), custom_call_target="InvertDiagBlocksLowerTriangular" | custom-call | tf_op jit(solution)/shard_map/jit(cholesky)/cholesky | solution.py:45
  332.3 11.7 %cholesky.217 = f32[128,128]{1,0:T(8,128)S(1)} custom-call(f32[128,128]{1,0:T(8,128)S(1)} %cholesky.270), custom_call_target="Cholesky" | custom-call | tf_op jit(solution)/shard_map/jit(cholesky)/cholesky | solution.py:45
  344.0 10.0 %custom-call.32 = f32[1,128,128]{1,2,0:T(8,128)S(1)} custom-call(f32[1,128,128]{2,1,0:T(8,128)S(1)} %get-tuple-element.34), custom_call_target="InvertDiagBlocksLowerTriangular" | custom-call | tf_op jit(solution)/shard_map/jit(cholesky)/cholesky | solution.py:45
  354.7 11.7 %cholesky.238 = f32[128,128]{1,0:T(8,128)S(1)} custom-call(f32[128,128]{1,0:T(8,128)S(1)} %cholesky.275), custom_call_target="Cholesky" | custom-call | tf_op jit(solution)/shard_map/jit(cholesky)/cholesky | solution.py:45
  367.1 9.8 %custom-call.33 = f32[1,128,128]{1,2,0:T(8,128)S(1)} custom-call(f32[1,128,128]{2,1,0:T(8,128)S(1)} %get-tuple-element.31), custom_call_target="InvertDiagBlocksLowerTriangular" | custom-call | tf_op jit(solution)/shard_map/jit(cholesky)/cholesky | solution.py:45
  377.5 11.7 %cholesky.255 = f32[128,128]{1,0:T(8,128)S(1)} custom-call(f32[128,128]{1,0:T(8,128)S(1)} %convolution_subtract_fusion.5), custom_call_target="Cholesky" | custom-call | tf_op jit(solution)/shard_map/jit(cholesky)/cholesky | solution.py:45
  393.5 10.3 %while.1 = (s32[]{:T(128)}, f32[512,512]{1,0:T(8,128)S(1)}, s32[4,2]{0,1:T(2,128)S(1)}, f32[4,128,128]{2,1,0:T(8,128)}, s32[]{:T(128)}) while((s32[]{:T(128)}, f32[512,512]{1,0:T(8,128)S(1)}, s32[4,2]{0,1:T(2,128)S(1)}, f32[4,128,128]{2,1,0:T(8,128)}, s32[]{:T(128)}) %tuple.33), condition=%wide.while_cond, body=%wide.while_body.sunk | while | flops 2 | bytes 132705 | solution.py:46
  394.1 2.0 bitcast_dynamic-update-slice_fusion.2
  396.7 2.0 bitcast_dynamic-update-slice_fusion.2
  399.2 2.0 bitcast_dynamic-update-slice_fusion.2
  401.8 2.0 bitcast_dynamic-update-slice_fusion.2
  403.8 40.1 %custom-call.34 = f32[4,128,128]{1,2,0:T(8,128)S(1)} custom-call(f32[4,128,128]{2,1,0:T(8,128)} %get-tuple-element.9), custom_call_target="InvertDiagBlocksLowerTriangular" | custom-call | tf_op jit(solution)/shard_map/jit(_solve_triangular)/triangular_solve | solution.py:46
  443.9 1.2 fusion.30
  448.4 1.6 copy.8
  450.0 1.8 fusion
  451.8 2.6 fusion.1
  454.4 2.8 fusion.36
  (68 shorter events, 18.8 us)
Async XLA Ops:
  7.2 0.7 copy-start.8
  7.2 297.7 %all-reduce.5.cloned.1.call-start = ((), (), s32[]{:S(2)}) async-start(), calls=%async_computation | async-start | bytes 4194304 | tf_op jit(solution)/shard_map/psum | solution.py:37
  7.8 11.2 %copy-start.4 = (bf16[1,256,512]{2,1,0:T(8,128)(2,1)S(1)}, bf16[1,256,512]{2,1,0:T(8,128)(2,1)}, u32[]{:S(2)}) copy-start(bf16[1,256,512]{2,1,0:T(8,128)(2,1)} %param.3) | copy-start | bytes 786436
  9.0 10.6 %collective-permute-start = (bf16[64,512]{1,0:T(8,128)(2,1)S(1)}, bf16[64,512]{1,0:T(8,128)(2,1)S(1)}, u32[]{:S(2)}, u32[]{:S(2)}) collective-permute-start(bf16[64,512]{1,0:T(8,128)(2,1)S(1)} %slice.134), channel_id=1, source_target_pairs={{1,0},{2,1},{3,2},{4,3},{5,4},{6,5},{7,6},{8,7},{9,8},{10,9},{11,1... | collective-permute-start | bytes 196616 | tf_op jit(solution)/shard_map/ppermute | solution.py:10
  306.9 1.2 copy-start
  308.9 1.0 copy-start.2
  309.9 21.7 %copy-start.3 = (f32[512,512]{1,0:T(8,128)S(1)}, f32[512,512]{1,0:T(8,128)}, u32[]{:S(2)}) copy-start(f32[512,512]{1,0:T(8,128)} %copy-done.2) | copy-start | bytes 3145732
  393.3 51.8 %copy-start.1 = (f32[512,512]{1,0:T(8,128)S(1)}, f32[512,512]{1,0:T(8,128)}, u32[]{:S(2)}) copy-start(f32[512,512]{1,0:T(8,128)} %fusion.21) | copy-start | bytes 3145732
  443.9 1.6 copy-start.6
  445.9 1.0 copy-start.7
  450.0 1.8 copy-start.5
Sparse Core Ops, SparseCore 0:
  22.5 282.3 all-reduce.4
where the time goes:
time: 467 us; the launch traced here: 465 us
  waiting for transfers between devices  176 us (38%)
  other arithmetic  126 us (27%)
  blocking collectives  103 us (22%)
  between operations  18.6 us (4%)
  matrix products  16.3 us (3%)
  local copies, waits for them, and re-layouts  15.4 us (3%)
  starting transfers between devices  8.82 us (2%)
    psum x1, waiting for transfers between devices, on_device(): lax.psum((samples, totals, instant, crossed), ('traj', 'blk'))  176 us
    psum x1, blocking collectives, on_device(): lax.psum((samples, totals, instant, crossed), ('traj', 'blk'))  103 us
    another operation x14, other arithmetic, on_device(): factor = jnp.linalg.cholesky(instant_cov)  78.8 us
    another operation x3, other arithmetic, on_device(): jax.scipy.linalg.solve_triangular(factor, jnp.eye(width, dtype=jnp.float3...  40.3 us
    another operation x12, local copies, waits for them, and re-layouts  10.3 us
  transfers between devices with their start and end apart: 2, of which 1 were waited for; matrix products, arithmetic and copies ran while one was open for 1% of the time, Pallas kernels for 0%

commit v1 on v0

v1 whole, which is shorter than its diff:
```python
import jax
import jax.numpy as jnp
from jax import lax
from jax.experimental import pallas as pl
from jax.experimental.pallas import tpu as pltpu
from jax.sharding import PartitionSpec as P

MESH = pl.DeviceIdType.MESH
LAG = 64
HALF = 576
PARTS = (
    (0, 256, "x", (("rs", "y"), ("ar", "z"), ("ag", "y"))),
    (256, 128, "y", (("ar", "z"), ("ar", "x"))),
    (384, 192, "z", (("ar", "x"), ("ar", "y"))),
)
SIZE = {"x": 4, "y": 8, "z": 8}
FAR = {4: (2, 1, 3), 8: (4, 3, 5, 2, 6, 1, 7)}
BLOCKS = (((0, 1), (1, 2)), ((0, 2), (1, 3)), ((0, 3), (2, 3)), ((0, 0), (2, 2)), ((1, 1), (3, 3)))


def all_steps(part):
    return (("rs", part[2]),) + part[3] + (("ag", part[2]),)


class Record:
    pass


class Place:
    def __init__(self):
        self.traj, self.blk = lax.axis_index("traj"), lax.axis_index("blk")
        self.core = lax.rem(self.blk, 2)
        self.chip = lax.div(self.blk, 2)
        self.at = {"x": lax.rem(self.chip, 4), "y": self.traj, "z": lax.div(self.blk, 8)}
        self.partner = (self.traj, self.blk + 1 - 2 * self.core)

    def device(self, axis, index):
        if axis == "x":
            return (self.traj, self.at["z"] * 8 + index * 2 + self.core)
        if axis == "y":
            return (index, self.blk)
        return (self.traj, index * 8 + self.at["x"] * 2 + self.core)


def remote(src, dst, send, recv, to):
    return pltpu.make_async_remote_copy(
        src_ref=src, dst_ref=dst, send_sem=send, recv_sem=recv, device_id=to, device_id_type=MESH
    )


class Stream:
    def __init__(self, place, acc, out, bufs, sums, send, recv, core_send, core_recv):
        self.place, self.acc, self.out = place, acc, out
        self.send, self.recv = send, recv
        self.core_send, self.core_recv = core_send, core_recv
        self.waiting, self.last, self.runs = [], [], []
        sem_at = buf_at = 0
        for part in PARTS:
            run = Record()
            run.base, run.rows = part[0], part[1]
            run.steps = []
            for kind, axis in all_steps(part):
                step = Record()
                step.kind, step.axis, step.sem = kind, axis, sem_at
                sem_at += SIZE[axis]
                if kind != "ag":
                    step.buf, step.sum = bufs[buf_at], sums[buf_at]
                    buf_at += 1
                run.steps.append(step)
            self.runs.append(run)
        self.n_steps = max(len(run.steps) for run in self.runs)

    def start(self):
        for run in self.runs:
            run.now, run.now_at, run.now_rows = self.acc, run.base, run.rows
            run.home = run.base
        for run in self.runs[::-1]:
            self.begin(run, 0)

    def advance(self, n):
        for k, run in enumerate(self.runs):
            if n < len(run.steps):
                self.finish(run, n)
                if n + 1 < len(run.steps):
                    self.begin(run, n + 1)
                else:
                    rows = self.out.at[self.place.core, pl.ds(run.base, run.rows)]
                    c = remote(rows, rows, self.core_send.at[k], self.core_recv.at[k], self.place.partner)
                    c.start()
                    self.last.append(c)

    def arrive(self):
        for c in self.last:
            c.wait_recv()

    def close(self):
        for c in self.waiting + self.last:
            c.wait_send()

    def begin(self, run, n):
        step = run.steps[n]
        axis, size = step.axis, SIZE[step.axis]
        me = self.place.at[axis]
        step.copies = {}
        for d in FAR[size]:
            to = lax.rem(me + d, size)
            if step.kind == "rs":
                rows = run.now_rows // size
                src = run.now.at[pl.ds(pl.multiple_of(run.now_at + to * rows, 8), rows)]
                dst, slot = step.buf.at[d - 1], d
            elif step.kind == "ar":
                src = run.now.at[pl.ds(run.now_at, run.now_rows)]
                dst, slot = step.buf.at[me], me
            else:
                src = dst = self.out.at[self.place.core, pl.ds(run.home, run.now_rows)]
                slot = d
            step.copies[d] = remote(
                src, dst, self.send.at[step.sem + d], self.recv.at[step.sem + slot], self.place.device(axis, to)
            )
            step.copies[d].start()
        if step.kind == "ar":
            step.buf[me] = run.now[pl.ds(run.now_at, run.now_rows)]
        self.waiting.extend(step.copies.values())

    def finish(self, run, n):
        step = run.steps[n]
        axis, size = step.axis, SIZE[step.axis]
        me = self.place.at[axis]
        near = FAR[size][::-1]
        if step.kind == "rs":
            rows = run.now_rows // size
            total = run.now[pl.ds(pl.multiple_of(run.now_at + me * rows, 8), rows)]
            for d in near:
                step.copies[d].wait_recv()
                total = total + step.buf[d - 1]
            step.sum[...] = total
            run.now, run.now_at, run.now_rows = step.sum, 0, rows
            run.home = run.home + me * rows
        elif step.kind == "ar":
            for d in near:
                come = lax.rem(me + d, size)
                remote(
                    run.now.at[pl.ds(run.now_at, run.now_rows)],
                    step.buf.at[come],
                    self.send.at[step.sem + d],
                    self.recv.at[step.sem + come],
                    self.place.device(axis, come),
                ).wait_recv()
            total = step.buf[0]
            for j in range(1, size):
                total = total + step.buf[j]
            step.sum[...] = total
            run.now, run.now_at = step.sum, 0
        else:
            for d in near:
                step.copies[d].wait_recv()
            run.home = run.home - me * run.now_rows
            run.now_rows = run.now_rows * size
        if n + 1 < len(run.steps) and run.steps[n + 1].kind == "ag":
            run.home = pl.multiple_of(run.home, 8)
            if step.kind != "ag":
                self.out[self.place.core, pl.ds(run.home, run.now_rows)] = run.now[...]


def moments_kernel(codes_ref, scale_ref, valid_ref, inst_ref, lag_ref, frames, turned, weighted, trailing, acc, *rest):
    (frame_send, frame_recv), rest = rest[:2], rest[2:]
    n = sum(kind != "ag" for part in PARTS for kind, _ in all_steps(part))
    place = Place()
    core = place.core
    streams = []
    for s, out in enumerate((inst_ref, lag_ref)):
        bufs, sums, sems = rest[:n], rest[n : 2 * n], rest[2 * n : 2 * n + 4]
        rest = rest[2 * n + 4 :]
        streams.append(Stream(place, acc.at[s], out, bufs, sums, *sems))
    instant, lagged = streams

    chips = 32
    before = lax.rem(place.chip + chips - 1, chips)
    after = lax.rem(place.chip + 1, chips)
    barrier = pltpu.get_barrier_semaphore()
    greeted = [place.partner, (place.traj, after * 2)]
    for axis, size in SIZE.items():
        greeted += [place.device(axis, lax.rem(place.at[axis] + d, size)) for d in range(1, size)]
    for device in greeted:
        pl.semaphore_signal(barrier, inc=1, device_id=device, device_id_type=MESH)

    rows_of = lax.broadcasted_iota(jnp.int32, (128, 128), 0)
    lanes_of = lax.broadcasted_iota(jnp.int32, (128, 128), 1)
    bf16, f32 = jnp.bfloat16, jnp.float32
    mine = pl.multiple_of(core * 256, 256)
    for i in range(2):
        scale = jnp.transpose(jnp.broadcast_to(scale_ref[:, 128 * i : 128 * i + 128], (128, 128)))
        at = pl.ds(pl.multiple_of(mine + 128 * i, 128), 128)
        for p in range(4):
            codes = codes_ref[128 * i : 128 * i + 128, 128 * p : 128 * p + 128]
            frames[p, at, :] = (codes.astype(f32) * scale).astype(bf16)

    pl.semaphore_wait(barrier, len(greeted) - 1 + 2 * (1 - core))
    own = frames.at[:, pl.ds(mine, 256), :]
    swap = remote(own, own, frame_send.at[0], frame_recv.at[0], place.partner)
    swap.start()
    first, halo = frames.at[:, pl.ds(0, LAG), :], frames.at[:, pl.ds(512, LAG), :]
    heads = [
        remote(first, halo, frame_send.at[1 + c], frame_recv.at[1], (place.traj, before * 2 + c)) for c in range(2)
    ]

    @pl.when(core == 0)
    def _():
        for c in heads:
            c.start()

    start = place.chip * 512
    valid = valid_ref[0]

    def prepare(block):
        at = pl.ds(pl.multiple_of(block * 128, 128), 128)
        t = rows_of + (start + block * 128)
        weight = jnp.where(t + LAG < valid, 1.0, 0.0) + jnp.where((t >= LAG) & (t < valid), 1.0, 0.0)
        for p in range(4):
            x = frames[p, at, :].astype(f32)
            turned[p, block] = jnp.transpose(x).astype(bf16)
            weighted[p, at, :] = (x * weight).astype(bf16)

    def block_of(k):
        (a0, b0), (a1, b1) = BLOCKS[k]
        return a0 + core * (a1 - a0), b0 + core * (b1 - b0)

    def product(a, right):
        return sum(
            dot(turned[a, i], right[128 * i : 128 * i + 128], ROWS, None) for i in range(4)
        )

    prepare(2 * core)
    prepare(2 * core + 1)
    swap.wait_recv()
    prepare(2 - 2 * core)
    prepare(3 - 2 * core)

    row8 = lax.broadcasted_iota(jnp.int32, (8, 128), 0)
    for k in range(3):
        a, b = block_of(k)
        acc[0, 128 * k : 128 * k + 128] = product(a, weighted[b])
    on = [product(block_of(k)[0], weighted[block_of(k)[0]]) for k in (3, 4)]
    acc[0, 384:512] = jnp.where(rows_of <= lanes_of, on[0], on[1])
    diagonal = jnp.sum(jnp.where(rows_of == lanes_of, on[1], 0.0), axis=0, keepdims=True)
    ones = jnp.ones((16, 512), bf16)
    totals = jnp.concatenate(
        [jnp.zeros((4, 128), f32)] + [dot(ones, weighted[p], ROWS, None)[:1] for p in range(4)], axis=0
    )
    count = jnp.clip(valid - LAG - start, 0, 512).astype(f32) * 2.0
    extra = jnp.where(core == 0, totals, jnp.full((8, 128), count))
    acc[0, 512:520] = jnp.where(row8 == 0, diagonal, extra)
    acc[0, 520:576] = jnp.zeros((56, 128), f32)
    instant.start()

    remote(first, halo, frame_send.at[1], frame_recv.at[1], (place.traj, after * 2)).wait_recv()
    for block in range(4):
        t = rows_of + (start + block * 128)
        for p in range(4):
            x = frames[p, 128 * block + LAG : 128 * block + LAG + 128, :].astype(f32)
            trailing[p, 128 * block : 128 * block + 128, :] = jnp.where(t + LAG < valid, x, 0.0).astype(bf16)
    for k in range(3):
        a, b = block_of(k)
        acc[1, 128 * k : 128 * k + 128] = product(b, trailing[a]) + jnp.transpose(product(a, trailing[b]))
    on = [product(block_of(k)[0], trailing[block_of(k)[0]]) for k in (3, 4)]
    on = [x + jnp.transpose(x) for x in on]
    acc[1, 384:512] = jnp.where(rows_of >= lanes_of, on[0], on[1])
    diagonal = jnp.sum(jnp.where(rows_of == lanes_of, on[1], 0.0), axis=0, keepdims=True)
    acc[1, 512:520] = jnp.where(row8 == 0, diagonal, 0.0)
    acc[1, 520:576] = jnp.zeros((56, 128), f32)

    instant.advance(0)
    lagged.start()
    for n in range(1, instant.n_steps):
        instant.advance(n)
        lagged.advance(n - 1)
    lagged.advance(lagged.n_steps - 1)
    instant.arrive()
    lagged.arrive()
    instant.close()
    lagged.close()
    swap.wait_send()

    @pl.when(core == 0)
    def _():
        for c in heads:
            c.wait_send()


def sum_scratch():
    bufs, sums, sems = [], [], 0
    for part in PARTS:
        rows = part[1]
        for kind, axis in all_steps(part):
            size = SIZE[axis]
            sems += size
            if kind == "rs":
                rows //= size
                bufs.append(pltpu.VMEM((size - 1, rows, 128), jnp.float32))
                sums.append(pltpu.VMEM((rows, 128), jnp.float32))
            elif kind == "ar":
                bufs.append(pltpu.VMEM((size, rows, 128), jnp.float32))
                sums.append(pltpu.VMEM((rows, 128), jnp.float32))
    return [
        *bufs,
        *sums,
        pltpu.SemaphoreType.DMA((sems,)),
        pltpu.SemaphoreType.DMA((sems,)),
        pltpu.SemaphoreType.DMA((len(PARTS),)),
        pltpu.SemaphoreType.DMA((len(PARTS),)),
    ]


def moments(codes, row_scale, valid):
    vmem = pl.BlockSpec(memory_space=pltpu.VMEM)
    out = jax.ShapeDtypeStruct((2, HALF, 128), jnp.float32)
    return pl.pallas_call(
        moments_kernel,
        out_shape=(out, out),
        in_specs=[vmem, vmem, pl.BlockSpec(memory_space=pltpu.SMEM)],
        out_specs=(vmem, vmem),
        scratch_shapes=[
            pltpu.VMEM((4, 512 + LAG, 128), jnp.bfloat16),
            pltpu.VMEM((4, 4, 128, 128), jnp.bfloat16),
            pltpu.VMEM((4, 512, 128), jnp.bfloat16),
            pltpu.VMEM((4, 512, 128), jnp.bfloat16),
            pltpu.VMEM((2, HALF, 128), jnp.float32),
            pltpu.SemaphoreType.DMA((3,)),
            pltpu.SemaphoreType.DMA((2,)),
            *sum_scratch(),
            *sum_scratch(),
        ],
        compiler_params=pltpu.CompilerParams(
            collective_id=0, has_side_effects=True, vmem_limit_bytes=40 * 2**20
        ),
        name="moments",
    )(codes, row_scale, valid)


HIGHEST = lax.Precision.HIGHEST
ROWS = (((1,), (0,)), ((), ()))
LANES = (((1,), (1,)), ((), ()))
SUBLANES = (((0,), (0,)), ((), ()))


def dot(left, right, dims, precision=HIGHEST):
    return lax.dot_general(left, right, dims, precision=precision, preferred_element_type=jnp.float32)


def one_row(x, k):
    return jnp.broadcast_to(x[k : k + 1, :], (8, 128))


def one_lane(x, k):
    return jnp.broadcast_to(x[:, k : k + 1], (8, 128))


def inverse_factor(block):
    rows = list(block)
    n, size = len(rows), 8
    sub = lax.broadcasted_iota(jnp.int32, (8, 128), 0)
    lane = lax.broadcasted_iota(jnp.int32, (8, 128), 1)
    pivots = [None] * n
    for group in range(0, n, size):
        end = group + size
        coming = [one_lane(rows[group], 8 * group + k) for k in range(8)]
        for r in range(group, end):
            first = 8 * r
            last = r == end - 1
            columns = [[coming[k]] + [one_lane(rows[q], first + k) for q in range(r + 1, end)] for k in range(8)]
            if not last:
                coming = [one_lane(rows[r + 1], first + 8 + k) for k in range(8)]
            inside = (lane >= first) & (lane < first + 8)
            panel = jnp.where(inside, jnp.where(lane - first == sub, 1.0, 0.0), rows[r])
            for q in range(r + 1, end):
                rows[q] = jnp.where(inside, 0.0, rows[q])
            for k in range(8):
                entry = one_row(columns[k][0], k)
                rough = pl.reciprocal(entry, approx=True)
                mend = 2.0 - entry * rough
                pivot = rough * mend
                pivots[r] = pivot if k == 0 else jnp.where(sub == k, pivot, pivots[r])
                below = jnp.where(sub > k, columns[k][0], 0.0)
                factor = [below * pivot] + [column * pivot for column in columns[k][1:]]
                for m in range(k + 1, 8):
                    entry = one_row(columns[k][0], m)
                    columns[m] = [columns[m][0] - ((below * entry) * rough) * mend] + [
                        x - f * entry for x, f in zip(columns[m][1:], factor[1:])
                    ]
                if not last:
                    coming = [coming[m] - factor[1] * one_row(columns[k][1], m) for m in range(8)]
                row = one_row(panel, k)
                panel = panel - factor[0] * row
                for q in range(r + 1, end):
                    rows[q] = rows[q] - factor[q - r] * row
            rows[r] = panel
        if end < n:
            done = jnp.concatenate(rows[group:end], axis=0)
            factors = jnp.concatenate([rows[r] * pivots[r] for r in range(group, end)], axis=0)
            down = lax.broadcasted_iota(jnp.int32, done.shape, 0) + 8 * group
            along = lax.broadcasted_iota(jnp.int32, done.shape, 1)
            done = jnp.where((along > down) & (along < 8 * end), 0.0, done)
            change = dot(factors, done, SUBLANES)
            inside = (lane >= 8 * group) & (lane < 8 * end)
            for q in range(end, n):
                rows[q] = jnp.where(inside, 0.0, rows[q]) - change[8 * q : 8 * q + 8]
    return [jnp.where(lane <= sub + 8 * q, rows[q], 0.0) * jnp.sqrt(pivots[q]) for q in range(n)]


def split3(x):
    high = x.astype(jnp.bfloat16)
    rest = x - high.astype(jnp.float32)
    middle = rest.astype(jnp.bfloat16)
    return high, middle, (rest - middle.astype(jnp.float32)).astype(jnp.bfloat16)


def at_block(i):
    return slice(128 * i, 128 * i + 128)


def finish_kernel(inst_ref, lag_ref, x_ref, white_ref, koop_ref, A, S, lhs):
    f32 = jnp.float32
    ri = lax.broadcasted_iota(jnp.int32, (128, 128), 0)
    ci = lax.broadcasted_iota(jnp.int32, (128, 128), 1)
    inv = 1.0 / inst_ref[1, 516:517, :]
    avg = [inst_ref[0, 516 + j : 517 + j, :] * inv for j in range(4)]
    avg_down = [jnp.transpose(jnp.broadcast_to(a, (128, 128))) for a in avg]

    def on_diagonal(ref, i):
        stored = ref[i // 2, 384:512] * inv
        turned = jnp.transpose(stored)
        if i % 2 == 0:
            return stored, turned, stored
        return turned, stored, ref[i // 2, 512:513] * inv

    for k, pair in enumerate(BLOCKS[:3]):
        for c, (i, j) in enumerate(pair):
            A[at_block(i), at_block(j)] = inst_ref[c, at_block(k)] * inv - avg_down[i] * avg[j]
            S[at_block(j), at_block(i)] = lag_ref[c, at_block(k)] * inv - avg_down[j] * avg[i]
    for i in range(4):
        outer = avg_down[i] * avg[i]
        own, turned, diagonal = on_diagonal(inst_ref, i)
        whole = jnp.where(ri < ci, own, jnp.where(ri > ci, turned, diagonal))
        A[at_block(i), at_block(i)] = whole - outer
        own, _, diagonal = on_diagonal(lag_ref, i)
        S[at_block(i), at_block(i)] = jnp.where(
            ri > ci, own - outer, jnp.where(ri == ci, 0.5 * (diagonal - outer), 0.0)
        )
    for k in range(4):
        V = [A[128*k+8*q:128*k+8*q+8, at_block(k)] for q in range(16)]
        W = jnp.concatenate(inverse_factor(V), axis=0)
        if k == 0:
            R = dot(W, A[at_block(0), 128:], ROWS)
            A[at_block(0), 128:] = R
        else:
            R = dot(W, A[at_block(k), :], ROWS)
            A[at_block(k), :] = R
        A[at_block(k), at_block(k)] = W
        if k < 3:
            Rr = A[at_block(k), 128*(k+1):]
            upd = dot(Rr, A[at_block(k), :], SUBLANES)
            A[128*(k+1):, at_block(k)] = -upd[:, at_block(k)]
            if k > 0:
                A[128*(k+1):, 0:128*k] = A[128*(k+1):, 0:128*k] - upd[:, 0:128*k]
            A[128*(k+1):, 128*(k+1):] = A[128*(k+1):, 128*(k+1):] - upd[:, 128*(k+1):]
    z = jnp.zeros((128,128), f32)
    A[at_block(0), at_block(1)] = z
    A[at_block(2), at_block(3)] = z
    S[at_block(0), at_block(1)] = z
    S[at_block(2), at_block(3)] = z
    a = [A[0:256, 0:256], A[256:512, 0:256], A[256:512, 256:512]]
    s = [S[0:256, 0:256], S[256:512, 0:256], S[256:512, 256:512]]
    x = x_ref[...]
    lhs[0:256, :] = x
    am = [jnp.concatenate([t[m] for t in [split3(q) for q in avg]], axis=1) for m in range(3)]
    lhs[256:272, :] = jnp.concatenate(am + [jnp.zeros((13, 512), jnp.bfloat16)], axis=0)
    y = [None, None]
    for t in split3(a[0]):
        v = dot(lhs[:, 0:256], t, LANES, None)
        y[0] = v if y[0] is None else y[0] + v
    for t, u in zip(split3(a[1]), split3(a[2])):
        v = dot(lhs[:, 0:256], t, LANES, None) + dot(lhs[:, 256:512], u, LANES, None)
        y[1] = v if y[1] is None else y[1] + v
    for h in range(2):
        m = y[h][256:257] + y[h][257:258] + y[h][258:259]
        white_ref[:, 256*h:256*h+256] = (y[h][0:256] - m).astype(jnp.bfloat16)
    nn = ROWS; nt = LANES
    t00 = dot(a[0], s[0], nn)
    t10 = dot(a[1], s[0], nn) + dot(a[2], s[1], nn)
    t11 = dot(a[2], s[2], nn)
    k00 = dot(t00, a[0], nt)
    k01 = dot(t00, a[1], nt)
    k10 = dot(t10, a[0], nt)
    k11 = dot(t10, a[1], nt) + dot(t11, a[2], nt)
    koop_ref[0:256, 0:256] = k00 + jnp.transpose(k00)
    koop_ref[256:512, 256:512] = k11 + jnp.transpose(k11)
    k10 = k10 + jnp.transpose(k01)
    koop_ref[256:512, 0:256] = k10
    koop_ref[0:256, 256:512] = jnp.transpose(k10)


def finish(instant, lagged, x):
    width = x.shape[1]
    return pl.pallas_call(
        finish_kernel,
        out_shape=(
            jax.ShapeDtypeStruct(x.shape, jnp.bfloat16),
            jax.ShapeDtypeStruct((width, width), jnp.float32),
        ),
        in_specs=[pl.BlockSpec(memory_space=pltpu.VMEM)] * 3,
        out_specs=(pl.BlockSpec(memory_space=pltpu.VMEM),) * 2,
        scratch_shapes=[
            pltpu.VMEM((width, width), jnp.float32),
            pltpu.VMEM((width, width), jnp.float32),
            pltpu.VMEM((x.shape[0] + 16, width), jnp.bfloat16),
        ],
        compiler_params=pltpu.CompilerParams(vmem_limit_bytes=40 * 2**20),
        name="finish",
    )(instant, lagged, x)


def on_device(codes, row_scale, valid):
    instant, lagged = moments(codes[0], row_scale, valid)
    dequant = (codes[0].astype(jnp.float32) * row_scale[0][:, None]).astype(jnp.bfloat16)
    projected, koopman = finish(instant, lagged, dequant)
    return (projected[None], koopman)


def solution(mesh):
    return jax.shard_map(
        on_device,
        mesh=mesh,
        in_specs=(P("traj", "blk", None), P("traj", "blk"), P("traj")),
        out_specs=(P("traj", "blk", None), P()),
        check_vma=False,
    )
```

time: 467 us -> 72.8 us (0.16)
  waiting for transfers between devices: 176 us -> 0 us
  other arithmetic: 126 us -> 1.13 us
  blocking collectives: 103 us -> 0 us
  Pallas kernels: 0 us -> 69.5 us
  between operations: 18.6 us -> 1.31 us
  matrix products: 16.3 us -> 0 us
  local copies, waits for them, and re-layouts: 15.4 us -> 0.68 us
  starting transfers between devices: 8.82 us -> 0 us
    psum x1 -> x0, waiting for transfers between devices: 176 us -> none  [on_device(): lax.psum((samples, totals, instant, crossed), ('traj', 'blk'))]
    another operation x17 -> x0, other arithmetic: 119 us -> none  [the longest x14 78.8 us: on_device(): factor = jnp.linalg.cholesky(instant_cov)]
    psum x1 -> x0, blocking collectives: 103 us -> none  [on_device(): lax.psum((samples, totals, instant, crossed), ('traj', 'blk'))]
    pallas_call x0 -> x2, Pallas kernels: none -> 69.5 us  [the longest x1 51.6 us: moments(): pl.pallas_call(moments_kernel, out_shape=(out, out), in_specs=[vmem, vmem...]
    dot_general x6 -> x0, matrix products: 10.5 us -> none  [the longest x3 3.3 us: gram_matrix(): lax.dot_general(left_rows, right_rows, (((0,), (0,)), ((), ())), preferre...]
    another operation x17 -> x0, local copies, waits for them, and re-layouts: 10.4 us -> none
    ppermute x1 -> x0, starting transfers between devices: 8.79 us -> none  [passed_along(): return lax.ppermute(shard, axis, pairs)]
    another operation x13 -> x0, matrix products: 5.75 us -> none  [the longest x7 3.88 us: on_device(): jax.scipy.linalg.solve_triangular(factor, jnp.eye(width, dtype=jnp.float3...]
  transfers between devices with their start and end apart: 2 -> 0, of which waited for: 1 -> 0; matrix products, arithmetic and copies ran while one was open for 1% -> 0% of each run, Pallas kernels for 0% -> 0%
where the time goes in v1:
time: 72.8 us; the launch traced here: 72.7 us
  Pallas kernels  69.5 us (95%)
  between operations  1.31 us (2%)
  other arithmetic  1.13 us (2%)
    pallas_call x1, Pallas kernels, moments(): pl.pallas_call(moments_kernel, out_shape=(out, out), in_specs=[vmem, vmem...  51.6 us
    pallas_call x1, Pallas kernels, finish(): pl.pallas_call(finish_kernel, out_shape=(jax.ShapeDtypeStruct(x.shape, jn...  18 us

profile of v1, /device:TPU:1, one launch (start us, length us, event | category | flops | bytes accessed | tf_op | source)
XLA Modules:
  0.0 72.7 jit_solution(4191420353666717804)
XLA Ops:
  1.3 0.0 copy-start.1
  1.3 0.7 copy-done.1
  2.0 0.0 copy-start
  2.0 1.1 %multiply_convert_fusion.x_ref = bf16[256,512]{1,0:T(8,128)(2,1)S(1)} fusion(f32[256]{0:T(256)S(1)} %bitcast.5, bf16[1,256,512]{2,1,0:T(8,128)(2,1)} %param.3), kind=kLoop, calls=%fused_computation | loop fusion | flops 393216 | bytes 525312 | tf_op jit(solution)/shard_map/convert_element_type | solution.py:524
  3.1 0.0 copy-done
  3.1 51.6 %moments.1 = (f32[2,576,128]{2,1,0:T(8,128)S(1)}, f32[2,576,128]{2,1,0:T(8,128)S(1)}) custom-call(bf16[256,512]{1,0:T(8,128)(2,1)S(1)} %bitcast.4, f32[1,256]{1,0:T(1,128)S(1)} %copy-done.1, s32[1]{0:T(128)S(6)} %copy.5.valid_ref), custom_call_target="tpu_custom_call" | custom-call | tf_op jit(solution)/shard_map/moments/pallas_call | solution.py:317
  54.7 18.0 %finish.1 = (bf16[256,512]{1,0:T(8,128)(2,1)}, f32[512,512]{1,0:T(8,128)}) custom-call(f32[2,576,128]{2,1,0:T(8,128)S(1)} %get-tuple-element.6.inst_ref, f32[2,576,128]{2,1,0:T(8,128)S(1)} %get-tuple-element.7.lag_ref, bf16[256,512]{1,0:T(8,128)(2,1)S(1)} %multiply_convert_fusion.x_ref), custom_call_target="tpu_custom_call" | custom-call | tf_op jit(solution)/shard_map/finish/pallas_call | solution.py:504
Async XLA Ops:
  1.3 0.7 copy-start.1
  2.0 1.1 %copy-start = (bf16[1,256,512]{2,1,0:T(8,128)(2,1)S(1)}, bf16[1,256,512]{2,1,0:T(8,128)(2,1)}, u32[]{:S(2)}) copy-start(bf16[1,256,512]{2,1,0:T(8,128)(2,1)} %param.3) | copy-start | bytes 786436

commit v2 on v1

--- a/solution.py
+++ b/solution.py
@@ -7,11 +7,11 @@
 
 MESH = pl.DeviceIdType.MESH
 LAG = 64
-HALF = 576
+HALF = 544
 PARTS = (
-    (0, 256, "x", (("rs", "y"), ("ar", "z"), ("ag", "y"))),
-    (256, 128, "y", (("ar", "z"), ("ar", "x"))),
-    (384, 192, "z", (("ar", "x"), ("ar", "y"))),
+    (0, 96, "x", (("ar", "y"), ("ar", "z"))),
+    (96, 192, "y", (("ar", "z"), ("ar", "x"))),
+    (288, 256, "z", (("ar", "x"), ("ar", "y"))),
 )
 SIZE = {"x": 4, "y": 8, "z": 8}
 FAR = {4: (2, 1, 3), 8: (4, 3, 5, 2, 6, 1, 7)}
@@ -162,13 +162,15 @@
                 self.out[self.place.core, pl.ds(run.home, run.now_rows)] = run.now[...]
 
 
-def moments_kernel(codes_ref, scale_ref, valid_ref, inst_ref, lag_ref, frames, turned, weighted, trailing, acc, *rest):
+def moments_kernel(
+    codes_ref, scale_ref, valid_ref, A, S, avg_ref, x_ref, frames, turned, weighted, trailing, acc, summed, *rest
+):
     (frame_send, frame_recv), rest = rest[:2], rest[2:]
     n = sum(kind != "ag" for part in PARTS for kind, _ in all_steps(part))
     place = Place()
     core = place.core
     streams = []
-    for s, out in enumerate((inst_ref, lag_ref)):
+    for s, out in enumerate((summed.at[0], summed.at[1])):
         bufs, sums, sems = rest[:n], rest[n : 2 * n], rest[2 * n : 2 * n + 4]
         rest = rest[2 * n + 4 :]
         streams.append(Stream(place, acc.at[s], out, bufs, sums, *sems))
@@ -193,7 +195,9 @@
         at = pl.ds(pl.multiple_of(mine + 128 * i, 128), 128)
         for p in range(4):
             codes = codes_ref[128 * i : 128 * i + 128, 128 * p : 128 * p + 128]
-            frames[p, at, :] = (codes.astype(f32) * scale).astype(bf16)
+            x = (codes.astype(f32) * scale).astype(bf16)
+            frames[p, at, :] = x
+            x_ref[128 * i : 128 * i + 128, 128 * p : 128 * p + 128] = x
 
     pl.semaphore_wait(barrier, len(greeted) - 1 + 2 * (1 - core))
     own = frames.at[:, pl.ds(mine, 256), :]
@@ -250,7 +254,7 @@
     count = jnp.clip(valid - LAG - start, 0, 512).astype(f32) * 2.0
     extra = jnp.where(core == 0, totals, jnp.full((8, 128), count))
     acc[0, 512:520] = jnp.where(row8 == 0, diagonal, extra)
-    acc[0, 520:576] = jnp.zeros((56, 128), f32)
+    acc[0, 520:HALF] = jnp.zeros((HALF - 520, 128), f32)
     instant.start()
 
     remote(first, halo, frame_send.at[1], frame_recv.at[1], (place.traj, after * 2)).wait_recv()
@@ -267,16 +271,27 @@
     acc[1, 384:512] = jnp.where(rows_of >= lanes_of, on[0], on[1])
     diagonal = jnp.sum(jnp.where(rows_of == lanes_of, on[1], 0.0), axis=0, keepdims=True)
     acc[1, 512:520] = jnp.where(row8 == 0, diagonal, 0.0)
-    acc[1, 520:576] = jnp.zeros((56, 128), f32)
+    acc[1, 520:HALF] = jnp.zeros((HALF - 520, 128), f32)
 
     instant.advance(0)
+    instant.advance(1)
     lagged.start()
-    for n in range(1, instant.n_steps):
-        instant.advance(n)
-        lagged.advance(n - 1)
-    lagged.advance(lagged.n_steps - 1)
+    instant.advance(2)
+    instant.advance(3)
     instant.arrive()
+    lagged.advance(0)
+    means = Means(summed.at[0], summed.at[1])
+    means.instant_cov(A)
+    D = A[at_block(0), at_block(0)]
+    for k in range(4):
+        D = eliminate(A, k, D)
+        if k < 3:
+            lagged.advance(k + 1)
+    A[at_block(0), at_block(1)] = jnp.zeros((128, 128), f32)
+    A[at_block(2), at_block(3)] = jnp.zeros((128, 128), f32)
+    avg_ref[...] = jnp.concatenate(means.avg + means.avg, axis=0)
     lagged.arrive()
+    means.lagged_cov(S)
     instant.close()
     lagged.close()
     swap.wait_send()
@@ -313,18 +328,20 @@
 
 def moments(codes, row_scale, valid):
     vmem = pl.BlockSpec(memory_space=pltpu.VMEM)
-    out = jax.ShapeDtypeStruct((2, HALF, 128), jnp.float32)
+    square = jax.ShapeDtypeStruct((codes.shape[1], codes.shape[1]), jnp.float32)
+    average = jax.ShapeDtypeStruct((8, 128), jnp.float32)
     return pl.pallas_call(
         moments_kernel,
-        out_shape=(out, out),
+        out_shape=(square, square, average, jax.ShapeDtypeStruct(codes.shape, codes.dtype)),
         in_specs=[vmem, vmem, pl.BlockSpec(memory_space=pltpu.SMEM)],
-        out_specs=(vmem, vmem),
+        out_specs=(vmem,) * 4,
         scratch_shapes=[
             pltpu.VMEM((4, 512 + LAG, 128), jnp.bfloat16),
             pltpu.VMEM((4, 4, 128, 128), jnp.bfloat16),
             pltpu.VMEM((4, 512, 128), jnp.bfloat16),
             pltpu.VMEM((4, 512, 128), jnp.bfloat16),
             pltpu.VMEM((2, HALF, 128), jnp.float32),
+            pltpu.VMEM((2, 2, HALF, 128), jnp.float32),
             pltpu.SemaphoreType.DMA((3,)),
             pltpu.SemaphoreType.DMA((2,)),
             *sum_scratch(),
@@ -360,10 +377,11 @@
     n, size = len(rows), 8
     sub = lax.broadcasted_iota(jnp.int32, (8, 128), 0)
     lane = lax.broadcasted_iota(jnp.int32, (8, 128), 1)
-    pivots = [None] * n
+    even = (sub % 2) == 0
     for group in range(0, n, size):
         end = group + size
         coming = [one_lane(rows[group], 8 * group + k) for k in range(8)]
+        pivots = []
         for r in range(group, end):
             first = 8 * r
             last = r == end - 1
@@ -374,37 +392,50 @@
             panel = jnp.where(inside, jnp.where(lane - first == sub, 1.0, 0.0), rows[r])
             for q in range(r + 1, end):
                 rows[q] = jnp.where(inside, 0.0, rows[q])
-            for k in range(8):
-                entry = one_row(columns[k][0], k)
-                rough = pl.reciprocal(entry, approx=True)
-                mend = 2.0 - entry * rough
-                pivot = rough * mend
-                pivots[r] = pivot if k == 0 else jnp.where(sub == k, pivot, pivots[r])
-                below = jnp.where(sub > k, columns[k][0], 0.0)
-                factor = [below * pivot] + [column * pivot for column in columns[k][1:]]
-                for m in range(k + 1, 8):
-                    entry = one_row(columns[k][0], m)
-                    columns[m] = [columns[m][0] - ((below * entry) * rough) * mend] + [
-                        x - f * entry for x, f in zip(columns[m][1:], factor[1:])
+            for k in range(0, 8, 2):
+                left, right = columns[k], columns[k + 1]
+                a, b, d = one_row(left[0], k), one_row(left[0], k + 1), one_row(right[0], k + 1)
+                det = a * d - b * b
+                rough = pl.reciprocal(det, approx=True)
+                mend = 2.0 - det * rough
+                inv = rough * mend
+                a_inv, b_inv, d_inv = a * inv, b * inv, d * inv
+                low, high = jnp.where(sub > k + 1, left[0], 0.0), jnp.where(sub > k + 1, right[0], 0.0)
+                g, h = low * d - high * b, high * a - low * b
+                f0 = [g * inv] + [x * d_inv - y * b_inv for x, y in zip(left[1:], right[1:])]
+                f1 = [h * inv] + [y * a_inv - x * b_inv for x, y in zip(left[1:], right[1:])]
+                for m in range(k + 2, 8):
+                    e0, e1 = one_row(left[0], m), one_row(right[0], m)
+                    columns[m] = [columns[m][0] - ((g * e0 + h * e1) * rough) * mend] + [
+                        x - (u * e0 + v * e1) for x, u, v in zip(columns[m][1:], f0[1:], f1[1:])
                     ]
                 if not last:
-                    coming = [coming[m] - factor[1] * one_row(columns[k][1], m) for m in range(8)]
-                row = one_row(panel, k)
-                panel = panel - factor[0] * row
+                    coming = [
+                        coming[m] - (f0[1] * one_row(left[1], m) + f1[1] * one_row(right[1], m)) for m in range(8)
+                    ]
+                row0, row1 = one_row(panel, k), one_row(panel, k + 1)
+                panel = panel - (f0[0] * row0 + f1[0] * row1)
                 for q in range(r + 1, end):
-                    rows[q] = rows[q] - factor[q - r] * row
+                    rows[q] = rows[q] - (f0[q - r] * row0 + f1[q - r] * row1)
+                if k == 0:
+                    pivot = (a, b, det)
+                else:
+                    pivot = tuple(jnp.where(sub >= k, x, y) for x, y in zip((a, b, det), pivot))
             rows[r] = panel
+            pivots.append(pivot)
+        for r in range(group, end):
+            a, b, det = pivots[r - group]
+            above = pltpu.roll(rows[r], 1, 0)
+            rows[r] = jnp.where(even, rows[r], rows[r] * a - above * b) * lax.rsqrt(jnp.where(even, a, a * det))
         if end < n:
             done = jnp.concatenate(rows[group:end], axis=0)
-            factors = jnp.concatenate([rows[r] * pivots[r] for r in range(group, end)], axis=0)
             down = lax.broadcasted_iota(jnp.int32, done.shape, 0) + 8 * group
             along = lax.broadcasted_iota(jnp.int32, done.shape, 1)
-            done = jnp.where((along > down) & (along < 8 * end), 0.0, done)
-            change = dot(factors, done, SUBLANES)
+            change = dot(done, jnp.where((along > down) & (along < 8 * end), 0.0, done), SUBLANES)
             inside = (lane >= 8 * group) & (lane < 8 * end)
             for q in range(end, n):
                 rows[q] = jnp.where(inside, 0.0, rows[q]) - change[8 * q : 8 * q + 8]
-    return [jnp.where(lane <= sub + 8 * q, rows[q], 0.0) * jnp.sqrt(pivots[q]) for q in range(n)]
+    return [jnp.where(lane <= sub + 8 * q, rows[q], 0.0) for q in range(n)]
 
 
 def split3(x):
@@ -418,56 +449,70 @@
     return slice(128 * i, 128 * i + 128)
 
 
-def finish_kernel(inst_ref, lag_ref, x_ref, white_ref, koop_ref, A, S, lhs):
-    f32 = jnp.float32
-    ri = lax.broadcasted_iota(jnp.int32, (128, 128), 0)
-    ci = lax.broadcasted_iota(jnp.int32, (128, 128), 1)
-    inv = 1.0 / inst_ref[1, 516:517, :]
-    avg = [inst_ref[0, 516 + j : 517 + j, :] * inv for j in range(4)]
-    avg_down = [jnp.transpose(jnp.broadcast_to(a, (128, 128))) for a in avg]
-
-    def on_diagonal(ref, i):
-        stored = ref[i // 2, 384:512] * inv
+def eliminate(A, k, D):
+    W = jnp.concatenate(inverse_factor([D[8 * q : 8 * q + 8, :] for q in range(16)]), axis=0)
+    A[at_block(k), at_block(k)] = W
+    if k < 3:
+        near = dot(W, A[at_block(k), at_block(k + 1)], ROWS)
+        D = A[at_block(k + 1), at_block(k + 1)] - dot(near, near, SUBLANES)
+        A[at_block(k), at_block(k + 1)] = near
+    for lo, hi in ((0, 128 * k), (128 * (k + 2), 512)):
+        if lo < hi:
+            A[at_block(k), lo:hi] = dot(W, A[at_block(k), lo:hi], ROWS)
+    if k < 3:
+        below = 128 * (k + 1)
+        change = dot(A[at_block(k), below:], A[at_block(k), :], SUBLANES)
+        A[below:, at_block(k)] = -change[:, at_block(k)]
+        if k > 0:
+            A[below:, 0 : 128 * k] = A[below:, 0 : 128 * k] - change[:, 0 : 128 * k]
+        if k < 2:
+            A[below:, below + 128 :] = A[below:, below + 128 :] - change[:, below + 128 :]
+    return D
+
+
+class Means:
+    def __init__(self, inst_ref, lag_ref):
+        self.inst, self.lag = inst_ref, lag_ref
+        self.inv = 1.0 / inst_ref[1, 516:517, :]
+        self.avg = [inst_ref[0, 516 + j : 517 + j, :] * self.inv for j in range(4)]
+        self.down = [jnp.transpose(jnp.broadcast_to(a, (128, 128))) for a in self.avg]
+        self.ri = lax.broadcasted_iota(jnp.int32, (128, 128), 0)
+        self.ci = lax.broadcasted_iota(jnp.int32, (128, 128), 1)
+
+    def on_diagonal(self, ref, i):
+        stored = ref[i // 2, 384:512] * self.inv
         turned = jnp.transpose(stored)
         if i % 2 == 0:
             return stored, turned, stored
-        return turned, stored, ref[i // 2, 512:513] * inv
-
-    for k, pair in enumerate(BLOCKS[:3]):
-        for c, (i, j) in enumerate(pair):
-            A[at_block(i), at_block(j)] = inst_ref[c, at_block(k)] * inv - avg_down[i] * avg[j]
-            S[at_block(j), at_block(i)] = lag_ref[c, at_block(k)] * inv - avg_down[j] * avg[i]
-    for i in range(4):
-        outer = avg_down[i] * avg[i]
-        own, turned, diagonal = on_diagonal(inst_ref, i)
-        whole = jnp.where(ri < ci, own, jnp.where(ri > ci, turned, diagonal))
-        A[at_block(i), at_block(i)] = whole - outer
-        own, _, diagonal = on_diagonal(lag_ref, i)
-        S[at_block(i), at_block(i)] = jnp.where(
-            ri > ci, own - outer, jnp.where(ri == ci, 0.5 * (diagonal - outer), 0.0)
-        )
-    for k in range(4):
-        V = [A[128*k+8*q:128*k+8*q+8, at_block(k)] for q in range(16)]
-        W = jnp.concatenate(inverse_factor(V), axis=0)
-        if k == 0:
-            R = dot(W, A[at_block(0), 128:], ROWS)
-            A[at_block(0), 128:] = R
-        else:
-            R = dot(W, A[at_block(k), :], ROWS)
-            A[at_block(k), :] = R
-        A[at_block(k), at_block(k)] = W
-        if k < 3:
-            Rr = A[at_block(k), 128*(k+1):]
-            upd = dot(Rr, A[at_block(k), :], SUBLANES)
-            A[128*(k+1):, at_block(k)] = -upd[:, at_block(k)]
-            if k > 0:
-                A[128*(k+1):, 0:128*k] = A[128*(k+1):, 0:128*k] - upd[:, 0:128*k]
-            A[128*(k+1):, 128*(k+1):] = A[128*(k+1):, 128*(k+1):] - upd[:, 128*(k+1):]
-    z = jnp.zeros((128,128), f32)
-    A[at_block(0), at_block(1)] = z
-    A[at_block(2), at_block(3)] = z
-    S[at_block(0), at_block(1)] = z
-    S[at_block(2), at_block(3)] = z
+        return turned, stored, ref[i // 2, 512:513] * self.inv
+
+    def instant_cov(self, A):
+        for k, pair in enumerate(BLOCKS[:3]):
+            for c, (i, j) in enumerate(pair):
+                A[at_block(i), at_block(j)] = self.inst[c, at_block(k)] * self.inv - self.down[i] * self.avg[j]
+        for i in range(4):
+            own, turned, diagonal = self.on_diagonal(self.inst, i)
+            whole = jnp.where(self.ri < self.ci, own, jnp.where(self.ri > self.ci, turned, diagonal))
+            A[at_block(i), at_block(i)] = whole - self.down[i] * self.avg[i]
+
+    def lagged_cov(self, S):
+        zero = jnp.zeros((128, 128), jnp.float32)
+        S[at_block(0), at_block(1)] = zero
+        S[at_block(2), at_block(3)] = zero
+        for k, pair in enumerate(BLOCKS[:3]):
+            for c, (i, j) in enumerate(pair):
+                S[at_block(j), at_block(i)] = self.lag[c, at_block(k)] * self.inv - self.down[j] * self.avg[i]
+        for i in range(4):
+            outer = self.down[i] * self.avg[i]
+            own, _, diagonal = self.on_diagonal(self.lag, i)
+            S[at_block(i), at_block(i)] = jnp.where(
+                self.ri > self.ci, own - outer, jnp.where(self.ri == self.ci, 0.5 * (diagonal - outer), 0.0)
+            )
+
+
+def finish_kernel(A, S, avg_ref, x_ref, white_ref, koop_ref, lhs):
+    f32 = jnp.float32
+    avg = [avg_ref[j : j + 1, :] for j in range(4)]
     a = [A[0:256, 0:256], A[256:512, 0:256], A[256:512, 256:512]]
     s = [S[0:256, 0:256], S[256:512, 0:256], S[256:512, 256:512]]
     x = x_ref[...]
@@ -499,7 +544,7 @@
     koop_ref[0:256, 256:512] = jnp.transpose(k10)
 
 
-def finish(instant, lagged, x):
+def finish(whitener, lagged_cov, average, x):
     width = x.shape[1]
     return pl.pallas_call(
         finish_kernel,
@@ -507,22 +552,16 @@
             jax.ShapeDtypeStruct(x.shape, jnp.bfloat16),
             jax.ShapeDtypeStruct((width, width), jnp.float32),
         ),
-        in_specs=[pl.BlockSpec(memory_space=pltpu.VMEM)] * 3,
+        in_specs=[pl.BlockSpec(memory_space=pltpu.VMEM)] * 4,
         out_specs=(pl.BlockSpec(memory_space=pltpu.VMEM),) * 2,
-        scratch_shapes=[
-            pltpu.VMEM((width, width), jnp.float32),
-            pltpu.VMEM((width, width), jnp.float32),
-            pltpu.VMEM((x.shape[0] + 16, width), jnp.bfloat16),
-        ],
+        scratch_shapes=[pltpu.VMEM((x.shape[0] + 16, width), jnp.bfloat16)],
         compiler_params=pltpu.CompilerParams(vmem_limit_bytes=40 * 2**20),
         name="finish",
-    )(instant, lagged, x)
+    )(whitener, lagged_cov, average, x)
 
 
 def on_device(codes, row_scale, valid):
-    instant, lagged = moments(codes[0], row_scale, valid)
-    dequant = (codes[0].astype(jnp.float32) * row_scale[0][:, None]).astype(jnp.bfloat16)
-    projected, koopman = finish(instant, lagged, dequant)
+    projected, koopman = finish(*moments(codes[0], row_scale, valid))
     return (projected[None], koopman)
 
 

time: 72.8 us -> 67.8 us (0.931)
  the two profiles are of different devices: /device:TPU:1 before, /device:TPU:7 now
where the time goes in v2:
time: 67.8 us; the launch traced here: 67.6 us
  Pallas kernels  64.7 us (95%)
  local copies, waits for them, and re-layouts  1.62 us (2%)
  between operations  1.29 us (2%)
    pallas_call x1, Pallas kernels, moments(): pl.pallas_call(moments_kernel, out_shape=(square, square, average, jax.Sh...  61 us
    pallas_call x1, Pallas kernels, finish(): pl.pallas_call(finish_kernel, out_shape=(jax.ShapeDtypeStruct(x.shape, jn...  3.71 us
    unnamed x4, local copies, waits for them, and re-layouts  1.62 us

profile of v2, /device:TPU:7, one launch (start us, length us, event | category | flops | bytes accessed | tf_op | source)
XLA Modules:
  0.0 67.6 jit_solution(11383282361384945862)
XLA Ops:
  1.3 0.0 copy-start.1
  1.3 0.7 copy-done.1
  2.0 0.0 copy-start
  2.0 0.9 %copy-done = bf16[1,256,512]{2,1,0:T(8,128)(2,1)S(1)} copy-done((bf16[1,256,512]{2,1,0:T(8,128)(2,1)S(1)}, bf16[1,256,512]{2,1,0:T(8,128)(2,1)}, u32[]{:S(2)}) %copy-start) | copy-done | bytes 262168
  2.9 61.0 %moments.1 = (f32[512,512]{1,0:T(8,128)S(1)}, f32[512,512]{1,0:T(8,128)S(1)}, f32[8,128]{1,0:T(8,128)S(1)}, bf16[256,512]{1,0:T(8,128)(2,1)S(1)}) custom-call(bf16[256,512]{1,0:T(8,128)(2,1)S(1)} %bitcast.2, f32[1,256]{1,0:T(1,128)S(1)} %copy-done.1, s32[1]{0:T(128)S(6)} %copy.5.valid_ref), custom_call_target="tpu_custom_call" | custom-call | tf_op jit(solution)/shard_map/moments/pallas_call | solution.py:333
  63.9 3.7 %finish.1 = (bf16[256,512]{1,0:T(8,128)(2,1)}, f32[512,512]{1,0:T(8,128)}) custom-call(f32[512,512]{1,0:T(8,128)S(1)} %get-tuple-element.8.A, f32[512,512]{1,0:T(8,128)S(1)} %get-tuple-element.9.S, f32[8,128]{1,0:T(8,128)S(1)} %get-tuple-element.10.avg_ref, bf16[256,512]{1,0:T(8,128)(2,1)S(1)} %get-tuple-element.11.x_ref), custom_call_target="tpu_custom_call" | custom-call | tf_op jit(solution)/shard_map/finish/pallas_call | solution.py:549
Async XLA Ops:
  1.3 0.7 %copy-start.1 = (f32[1,256]{1,0:T(1,128)S(1)}, f32[1,256]{1,0:T(1,128)}, u32[]{:S(2)}) copy-start(f32[1,256]{1,0:T(1,128)} %scale_ref.1) | copy-start | bytes 3076
  2.0 0.9 %copy-start = (bf16[1,256,512]{2,1,0:T(8,128)(2,1)S(1)}, bf16[1,256,512]{2,1,0:T(8,128)(2,1)}, u32[]{:S(2)}) copy-start(bf16[1,256,512]{2,1,0:T(8,128)(2,1)} %param.3) | copy-start | bytes 786436

commit v3 on v2

--- a/solution.py
+++ b/solution.py
@@ -15,7 +15,8 @@
 )
 SIZE = {"x": 4, "y": 8, "z": 8}
 FAR = {4: (2, 1, 3), 8: (4, 3, 5, 2, 6, 1, 7)}
-BLOCKS = (((0, 1), (1, 2)), ((0, 2), (1, 3)), ((0, 3), (2, 3)), ((0, 0), (2, 2)), ((1, 1), (3, 3)))
+UPPER = (((0, 1), (2, 1)), ((0, 2), (2, 3)), ((0, 3), (3, 1)))
+BLOCKS = (((0, 1), (1, 2)), ((0, 2), (1, 3)), ((0, 3), (2, 3)))
 
 
 def all_steps(part):
@@ -163,10 +164,16 @@
 
 
 def moments_kernel(
-    codes_ref, scale_ref, valid_ref, A, S, avg_ref, x_ref, frames, turned, weighted, trailing, acc, summed, *rest
+    codes_in, scale_in, valid_ref, A, S, avg_ref, x_ref, codes_ref, scale_ref, load_sem, frames, turned, weighted, trailing, acc, summed, *rest
 ):
     (frame_send, frame_recv), rest = rest[:2], rest[2:]
     n = sum(kind != "ag" for part in PARTS for kind, _ in all_steps(part))
+    loads = [
+        pltpu.make_async_copy(scale_in, scale_ref, load_sem.at[0]),
+        pltpu.make_async_copy(codes_in, codes_ref, load_sem.at[1]),
+    ]
+    for load in loads:
+        load.start()
     place = Place()
     core = place.core
     streams = []
@@ -190,6 +197,8 @@
     lanes_of = lax.broadcasted_iota(jnp.int32, (128, 128), 1)
     bf16, f32 = jnp.bfloat16, jnp.float32
     mine = pl.multiple_of(core * 256, 256)
+    for load in loads:
+        load.wait()
     for i in range(2):
         scale = jnp.transpose(jnp.broadcast_to(scale_ref[:, 128 * i : 128 * i + 128], (128, 128)))
         at = pl.ds(pl.multiple_of(mine + 128 * i, 128), 128)
@@ -216,23 +225,24 @@
     start = place.chip * 512
     valid = valid_ref[0]
 
+    def rows_at(block):
+        return pl.ds(pl.multiple_of(block * 128, 128), 128)
+
+    def turn(block, panels):
+        for p in panels:
+            turned[p, block] = jnp.transpose(frames[p, rows_at(block), :].astype(f32)).astype(bf16)
+
     def prepare(block):
-        at = pl.ds(pl.multiple_of(block * 128, 128), 128)
         t = rows_of + (start + block * 128)
         weight = jnp.where(t + LAG < valid, 1.0, 0.0) + jnp.where((t >= LAG) & (t < valid), 1.0, 0.0)
         for p in range(4):
-            x = frames[p, at, :].astype(f32)
-            turned[p, block] = jnp.transpose(x).astype(bf16)
-            weighted[p, at, :] = (x * weight).astype(bf16)
-
-    def block_of(k):
-        (a0, b0), (a1, b1) = BLOCKS[k]
-        return a0 + core * (a1 - a0), b0 + core * (b1 - b0)
-
-    def product(a, right):
-        return sum(
-            dot(turned[a, i], right[128 * i : 128 * i + 128], ROWS, None) for i in range(4)
-        )
+            weighted[p, rows_at(block), :] = (frames[p, rows_at(block), :].astype(f32) * weight).astype(bf16)
+        turn(block, (2 * core, 2 * core + 1))
+
+    def product(a, *rights):
+        left = jnp.concatenate([turned[a, i] for i in range(4)], axis=1)
+        full = dot(left, jnp.concatenate([right[...] for right in rights], axis=1), ROWS, None)
+        return [full[:, at_block(k)] for k in range(len(rights))]
 
     prepare(2 * core)
     prepare(2 * core + 1)
@@ -241,10 +251,13 @@
     prepare(3 - 2 * core)
 
     row8 = lax.broadcasted_iota(jnp.int32, (8, 128), 0)
-    for k in range(3):
-        a, b = block_of(k)
-        acc[0, 128 * k : 128 * k + 128] = product(a, weighted[b])
-    on = [product(block_of(k)[0], weighted[block_of(k)[0]]) for k in (3, 4)]
+    first_core = core == 0
+    upper = product(2 * core, *[weighted.at[p] for p in range(4)])
+    lower = product(2 * core + 1, weighted.at[1], weighted.at[3])
+    acc[0, at_block(0)] = upper[1]
+    acc[0, at_block(1)] = jnp.where(first_core, upper[2], upper[3])
+    acc[0, at_block(2)] = jnp.where(first_core, upper[3], lower[0])
+    on = [jnp.where(first_core, upper[0], upper[2]), jnp.where(first_core, lower[0], lower[1])]
     acc[0, 384:512] = jnp.where(rows_of <= lanes_of, on[0], on[1])
     diagonal = jnp.sum(jnp.where(rows_of == lanes_of, on[1], 0.0), axis=0, keepdims=True)
     ones = jnp.ones((16, 512), bf16)
@@ -263,10 +276,13 @@
         for p in range(4):
             x = frames[p, 128 * block + LAG : 128 * block + LAG + 128, :].astype(f32)
             trailing[p, 128 * block : 128 * block + 128, :] = jnp.where(t + LAG < valid, x, 0.0).astype(bf16)
+    for block in range(4):
+        turn(block, (2 - 2 * core, 3 - 2 * core))
+    full = [product(a, *[trailing.at[b] for b in range(4)]) for a in range(4)]
     for k in range(3):
-        a, b = block_of(k)
-        acc[1, 128 * k : 128 * k + 128] = product(b, trailing[a]) + jnp.transpose(product(a, trailing[b]))
-    on = [product(block_of(k)[0], trailing[block_of(k)[0]]) for k in (3, 4)]
+        pair = [full[b][a] + jnp.transpose(full[a][b]) for a, b in BLOCKS[k]]
+        acc[1, at_block(k)] = jnp.where(first_core, *pair)
+    on = [jnp.where(first_core, full[i][i], full[i + 2][i + 2]) for i in range(2)]
     on = [x + jnp.transpose(x) for x in on]
     acc[1, 384:512] = jnp.where(rows_of >= lanes_of, on[0], on[1])
     diagonal = jnp.sum(jnp.where(rows_of == lanes_of, on[1], 0.0), axis=0, keepdims=True)
@@ -274,19 +290,20 @@
     acc[1, 520:HALF] = jnp.zeros((HALF - 520, 128), f32)
 
     instant.advance(0)
+    lagged.start()
     instant.advance(1)
-    lagged.start()
     instant.advance(2)
+    lagged.advance(0)
     instant.advance(3)
+    lagged.advance(1)
     instant.arrive()
-    lagged.advance(0)
     means = Means(summed.at[0], summed.at[1])
     means.instant_cov(A)
     D = A[at_block(0), at_block(0)]
-    for k in range(4):
-        D = eliminate(A, k, D)
-        if k < 3:
-            lagged.advance(k + 1)
+    D = eliminate(A, 0, D)
+    D = eliminate(A, 1, D, lambda: lagged.advance(2))
+    D = eliminate(A, 2, D)
+    eliminate(A, 3, D, lambda: lagged.advance(3))
     A[at_block(0), at_block(1)] = jnp.zeros((128, 128), f32)
     A[at_block(2), at_block(3)] = jnp.zeros((128, 128), f32)
     avg_ref[...] = jnp.concatenate(means.avg + means.avg, axis=0)
@@ -328,14 +345,18 @@
 
 def moments(codes, row_scale, valid):
     vmem = pl.BlockSpec(memory_space=pltpu.VMEM)
+    hbm = pl.BlockSpec(memory_space=pltpu.HBM)
     square = jax.ShapeDtypeStruct((codes.shape[1], codes.shape[1]), jnp.float32)
     average = jax.ShapeDtypeStruct((8, 128), jnp.float32)
     return pl.pallas_call(
         moments_kernel,
         out_shape=(square, square, average, jax.ShapeDtypeStruct(codes.shape, codes.dtype)),
-        in_specs=[vmem, vmem, pl.BlockSpec(memory_space=pltpu.SMEM)],
+        in_specs=[hbm, hbm, pl.BlockSpec(memory_space=pltpu.SMEM)],
         out_specs=(vmem,) * 4,
         scratch_shapes=[
+            pltpu.VMEM(codes.shape, codes.dtype),
+            pltpu.VMEM(row_scale.shape, row_scale.dtype),
+            pltpu.SemaphoreType.DMA((2,)),
             pltpu.VMEM((4, 512 + LAG, 128), jnp.bfloat16),
             pltpu.VMEM((4, 4, 128, 128), jnp.bfloat16),
             pltpu.VMEM((4, 512, 128), jnp.bfloat16),
@@ -372,7 +393,7 @@
     return jnp.broadcast_to(x[:, k : k + 1], (8, 128))
 
 
-def inverse_factor(block):
+def inverse_factor(block, halfway=None):
     rows = list(block)
     n, size = len(rows), 8
     sub = lax.broadcasted_iota(jnp.int32, (8, 128), 0)
@@ -435,6 +456,8 @@
             inside = (lane >= 8 * group) & (lane < 8 * end)
             for q in range(end, n):
                 rows[q] = jnp.where(inside, 0.0, rows[q]) - change[8 * q : 8 * q + 8]
+            if halfway is not None:
+                halfway()
     return [jnp.where(lane <= sub + 8 * q, rows[q], 0.0) for q in range(n)]
 
 
@@ -449,8 +472,8 @@
     return slice(128 * i, 128 * i + 128)
 
 
-def eliminate(A, k, D):
-    W = jnp.concatenate(inverse_factor([D[8 * q : 8 * q + 8, :] for q in range(16)]), axis=0)
+def eliminate(A, k, D, halfway=None):
+    W = jnp.concatenate(inverse_factor([D[8 * q : 8 * q + 8, :] for q in range(16)], halfway), axis=0)
     A[at_block(k), at_block(k)] = W
     if k < 3:
         near = dot(W, A[at_block(k), at_block(k + 1)], ROWS)
@@ -487,9 +510,13 @@
         return turned, stored, ref[i // 2, 512:513] * self.inv
 
     def instant_cov(self, A):
-        for k, pair in enumerate(BLOCKS[:3]):
+        for k, pair in enumerate(UPPER):
             for c, (i, j) in enumerate(pair):
-                A[at_block(i), at_block(j)] = self.inst[c, at_block(k)] * self.inv - self.down[i] * self.avg[j]
+                block = self.inst[c, at_block(k)] * self.inv - self.down[i] * self.avg[j]
+                if i < j:
+                    A[at_block(i), at_block(j)] = block
+                else:
+                    A[at_block(j), at_block(i)] = jnp.transpose(block)
         for i in range(4):
             own, turned, diagonal = self.on_diagonal(self.inst, i)
             whole = jnp.where(self.ri < self.ci, own, jnp.where(self.ri > self.ci, turned, diagonal))
@@ -499,7 +526,7 @@
         zero = jnp.zeros((128, 128), jnp.float32)
         S[at_block(0), at_block(1)] = zero
         S[at_block(2), at_block(3)] = zero
-        for k, pair in enumerate(BLOCKS[:3]):
+        for k, pair in enumerate(BLOCKS):
             for c, (i, j) in enumerate(pair):
                 S[at_block(j), at_block(i)] = self.lag[c, at_block(k)] * self.inv - self.down[j] * self.avg[i]
         for i in range(4):

time: 67.8 us -> 63.2 us (0.932)
  the two profiles are of different devices: /device:TPU:7 before, /device:TPU:1 now
where the time goes in v3:
time: 63.2 us; the launch traced here: 63 us
  Pallas kernels  60.1 us (95%)
  local copies, waits for them, and re-layouts  1.62 us (3%)
  between operations  1.29 us (2%)
    pallas_call x1, Pallas kernels, moments(): pl.pallas_call(moments_kernel, out_shape=(square, square, average, jax.Sh...  56.4 us
    pallas_call x1, Pallas kernels, finish(): pl.pallas_call(finish_kernel, out_shape=(jax.ShapeDtypeStruct(x.shape, jn...  3.71 us
    unnamed x4, local copies, waits for them, and re-layouts  1.62 us

profile of v3, /device:TPU:1, one launch (start us, length us, event | category | flops | bytes accessed | tf_op | source)
XLA Modules:
  0.0 63.0 jit_solution(2333137935414458621)
XLA Ops:
  1.3 0.0 copy-start.1
  1.3 0.7 %copy-done.1 = f32[1,256]{1,0:T(1,128)S(1)} copy-done((f32[1,256]{1,0:T(1,128)S(1)}, f32[1,256]{1,0:T(1,128)}, u32[]{:S(2)}) %copy-start.1) | copy-done | bytes 1048
  2.0 0.0 copy-start
  2.0 0.9 %copy-done = bf16[1,256,512]{2,1,0:T(8,128)(2,1)S(1)} copy-done((bf16[1,256,512]{2,1,0:T(8,128)(2,1)S(1)}, bf16[1,256,512]{2,1,0:T(8,128)(2,1)}, u32[]{:S(2)}) %copy-start) | copy-done | bytes 262168
  2.9 56.4 %moments.1 = (f32[512,512]{1,0:T(8,128)S(1)}, f32[512,512]{1,0:T(8,128)S(1)}, f32[8,128]{1,0:T(8,128)S(1)}, bf16[256,512]{1,0:T(8,128)(2,1)S(1)}) custom-call(bf16[256,512]{1,0:T(8,128)(2,1)S(1)} %bitcast.2, f32[1,256]{1,0:T(1,128)S(1)} %copy-done.1, s32[1]{0:T(128)S(6)} %copy.5.valid_ref), custom_call_target="tpu_custom_call" | custom-call | tf_op jit(solution)/shard_map/moments/pallas_call | solution.py:351
  59.3 3.7 %finish.1 = (bf16[256,512]{1,0:T(8,128)(2,1)}, f32[512,512]{1,0:T(8,128)}) custom-call(f32[512,512]{1,0:T(8,128)S(1)} %get-tuple-element.8.A, f32[512,512]{1,0:T(8,128)S(1)} %get-tuple-element.9.S, f32[8,128]{1,0:T(8,128)S(1)} %get-tuple-element.10.avg_ref, bf16[256,512]{1,0:T(8,128)(2,1)S(1)} %get-tuple-element.11.x_ref), custom_call_target="tpu_custom_call" | custom-call | tf_op jit(solution)/shard_map/finish/pallas_call | solution.py:576
Async XLA Ops:
  1.3 0.7 %copy-start.1 = (f32[1,256]{1,0:T(1,128)S(1)}, f32[1,256]{1,0:T(1,128)}, u32[]{:S(2)}) copy-start(f32[1,256]{1,0:T(1,128)} %scale_in.1) | copy-start | bytes 3076
  2.0 0.9 %copy-start = (bf16[1,256,512]{2,1,0:T(8,128)(2,1)S(1)}, bf16[1,256,512]{2,1,0:T(8,128)(2,1)}, u32[]{:S(2)}) copy-start(bf16[1,256,512]{2,1,0:T(8,128)(2,1)} %param.3) | copy-start | bytes 786436

commit v4 on v3

--- a/solution.py
+++ b/solution.py
@@ -7,11 +7,11 @@
 
 MESH = pl.DeviceIdType.MESH
 LAG = 64
-HALF = 544
+HALF = 576
 PARTS = (
-    (0, 96, "x", (("ar", "y"), ("ar", "z"))),
-    (96, 192, "y", (("ar", "z"), ("ar", "x"))),
-    (288, 256, "z", (("ar", "x"), ("ar", "y"))),
+    (0, 128, "x", (("ar", "y"), ("ar", "z"))),
+    (128, 256, "y", (("ar", "z"), ("ar", "x"))),
+    (384, 192, "z", (("ar", "x"), ("ar", "y"))),
 )
 SIZE = {"x": 4, "y": 8, "z": 8}
 FAR = {4: (2, 1, 3), 8: (4, 3, 5, 2, 6, 1, 7)}
@@ -54,7 +54,7 @@
         self.place, self.acc, self.out = place, acc, out
         self.send, self.recv = send, recv
         self.core_send, self.core_recv = core_send, core_recv
-        self.waiting, self.last, self.runs = [], [], []
+        self.waiting, self.last, self.runs = [], {}, []
         sem_at = buf_at = 0
         for part in PARTS:
             run = Record()
@@ -78,8 +78,9 @@
         for run in self.runs[::-1]:
             self.begin(run, 0)
 
-    def advance(self, n):
-        for k, run in enumerate(self.runs):
+    def advance(self, n, parts=(2, 0, 1)):
+        for k in parts:
+            run = self.runs[k]
             if n < len(run.steps):
                 self.finish(run, n)
                 if n + 1 < len(run.steps):
@@ -88,14 +89,14 @@
                     rows = self.out.at[self.place.core, pl.ds(run.base, run.rows)]
                     c = remote(rows, rows, self.core_send.at[k], self.core_recv.at[k], self.place.partner)
                     c.start()
-                    self.last.append(c)
-
-    def arrive(self):
-        for c in self.last:
-            c.wait_recv()
+                    self.last[k] = c
+
+    def arrive(self, parts=(0, 1, 2)):
+        for k in parts:
+            self.last[k].wait_recv()
 
     def close(self):
-        for c in self.waiting + self.last:
+        for c in self.waiting + list(self.last.values()):
             c.wait_send()
 
     def begin(self, run, n):
@@ -164,7 +165,7 @@
 
 
 def moments_kernel(
-    codes_in, scale_in, valid_ref, A, S, avg_ref, x_ref, codes_ref, scale_ref, load_sem, frames, turned, weighted, trailing, acc, summed, *rest
+    codes_in, scale_in, valid_ref, A, S, white_ref, codes_ref, scale_ref, load_sem, lhs, frames, turned, weighted, trailing, acc, summed, *rest
 ):
     (frame_send, frame_recv), rest = rest[:2], rest[2:]
     n = sum(kind != "ag" for part in PARTS for kind, _ in all_steps(part))
@@ -206,7 +207,7 @@
             codes = codes_ref[128 * i : 128 * i + 128, 128 * p : 128 * p + 128]
             x = (codes.astype(f32) * scale).astype(bf16)
             frames[p, at, :] = x
-            x_ref[128 * i : 128 * i + 128, 128 * p : 128 * p + 128] = x
+            lhs[128 * i : 128 * i + 128, 128 * p : 128 * p + 128] = x
 
     pl.semaphore_wait(barrier, len(greeted) - 1 + 2 * (1 - core))
     own = frames.at[:, pl.ds(mine, 256), :]
@@ -294,19 +295,26 @@
     instant.advance(1)
     instant.advance(2)
     lagged.advance(0)
-    instant.advance(3)
-    lagged.advance(1)
-    instant.arrive()
+    instant.advance(3, (2,))
+    instant.arrive((2,))
     means = Means(summed.at[0], summed.at[1])
-    means.instant_cov(A)
-    D = A[at_block(0), at_block(0)]
-    D = eliminate(A, 0, D)
+    means.instant_diagonal(A)
+
+    def rest():
+        instant.advance(3, (0, 1))
+        lagged.advance(1)
+
+    def upper_blocks():
+        instant.arrive((0, 1))
+        means.instant_cov(A)
+
+    D = eliminate(A, 0, A[at_block(0), at_block(0)], rest, upper_blocks)
     D = eliminate(A, 1, D, lambda: lagged.advance(2))
     D = eliminate(A, 2, D)
     eliminate(A, 3, D, lambda: lagged.advance(3))
     A[at_block(0), at_block(1)] = jnp.zeros((128, 128), f32)
     A[at_block(2), at_block(3)] = jnp.zeros((128, 128), f32)
-    avg_ref[...] = jnp.concatenate(means.avg + means.avg, axis=0)
+    whiten(A, means.avg, lhs, white_ref)
     lagged.arrive()
     means.lagged_cov(S)
     instant.close()
@@ -347,16 +355,16 @@
     vmem = pl.BlockSpec(memory_space=pltpu.VMEM)
     hbm = pl.BlockSpec(memory_space=pltpu.HBM)
     square = jax.ShapeDtypeStruct((codes.shape[1], codes.shape[1]), jnp.float32)
-    average = jax.ShapeDtypeStruct((8, 128), jnp.float32)
     return pl.pallas_call(
         moments_kernel,
-        out_shape=(square, square, average, jax.ShapeDtypeStruct(codes.shape, codes.dtype)),
+        out_shape=(square, square, jax.ShapeDtypeStruct(codes.shape, codes.dtype)),
         in_specs=[hbm, hbm, pl.BlockSpec(memory_space=pltpu.SMEM)],
-        out_specs=(vmem,) * 4,
+        out_specs=(vmem,) * 3,
         scratch_shapes=[
             pltpu.VMEM(codes.shape, codes.dtype),
             pltpu.VMEM(row_scale.shape, row_scale.dtype),
             pltpu.SemaphoreType.DMA((2,)),
+            pltpu.VMEM((codes.shape[0] + 16, codes.shape[1]), jnp.bfloat16),
             pltpu.VMEM((4, 512 + LAG, 128), jnp.bfloat16),
             pltpu.VMEM((4, 4, 128, 128), jnp.bfloat16),
             pltpu.VMEM((4, 512, 128), jnp.bfloat16),
@@ -472,8 +480,10 @@
     return slice(128 * i, 128 * i + 128)
 
 
-def eliminate(A, k, D, halfway=None):
+def eliminate(A, k, D, halfway=None, others=None):
     W = jnp.concatenate(inverse_factor([D[8 * q : 8 * q + 8, :] for q in range(16)], halfway), axis=0)
+    if others is not None:
+        others()
     A[at_block(k), at_block(k)] = W
     if k < 3:
         near = dot(W, A[at_block(k), at_block(k + 1)], ROWS)
@@ -517,6 +527,8 @@
                     A[at_block(i), at_block(j)] = block
                 else:
                     A[at_block(j), at_block(i)] = jnp.transpose(block)
+
+    def instant_diagonal(self, A):
         for i in range(4):
             own, turned, diagonal = self.on_diagonal(self.inst, i)
             whole = jnp.where(self.ri < self.ci, own, jnp.where(self.ri > self.ci, turned, diagonal))
@@ -537,13 +549,8 @@
             )
 
 
-def finish_kernel(A, S, avg_ref, x_ref, white_ref, koop_ref, lhs):
-    f32 = jnp.float32
-    avg = [avg_ref[j : j + 1, :] for j in range(4)]
+def whiten(A, avg, lhs, white_ref):
     a = [A[0:256, 0:256], A[256:512, 0:256], A[256:512, 256:512]]
-    s = [S[0:256, 0:256], S[256:512, 0:256], S[256:512, 256:512]]
-    x = x_ref[...]
-    lhs[0:256, :] = x
     am = [jnp.concatenate([t[m] for t in [split3(q) for q in avg]], axis=1) for m in range(3)]
     lhs[256:272, :] = jnp.concatenate(am + [jnp.zeros((13, 512), jnp.bfloat16)], axis=0)
     y = [None, None]
@@ -556,6 +563,13 @@
     for h in range(2):
         m = y[h][256:257] + y[h][257:258] + y[h][258:259]
         white_ref[:, 256*h:256*h+256] = (y[h][0:256] - m).astype(jnp.bfloat16)
+
+
+def finish_kernel(A, S, white_in, white_ref, koop_ref, sem):
+    handed_on = pltpu.make_async_copy(white_in, white_ref, sem)
+    handed_on.start()
+    a = [A[0:256, 0:256], A[256:512, 0:256], A[256:512, 256:512]]
+    s = [S[0:256, 0:256], S[256:512, 0:256], S[256:512, 256:512]]
     nn = ROWS; nt = LANES
     t00 = dot(a[0], s[0], nn)
     t10 = dot(a[1], s[0], nn) + dot(a[2], s[1], nn)
@@ -569,22 +583,22 @@
     k10 = k10 + jnp.transpose(k01)
     koop_ref[256:512, 0:256] = k10
     koop_ref[0:256, 256:512] = jnp.transpose(k10)
-
-
-def finish(whitener, lagged_cov, average, x):
-    width = x.shape[1]
+    handed_on.wait()
+
+
+def finish(whitener, lagged_cov, whitened):
     return pl.pallas_call(
         finish_kernel,
         out_shape=(
-            jax.ShapeDtypeStruct(x.shape, jnp.bfloat16),
-            jax.ShapeDtypeStruct((width, width), jnp.float32),
+            jax.ShapeDtypeStruct(whitened.shape, whitened.dtype),
+            jax.ShapeDtypeStruct(whitener.shape, jnp.float32),
         ),
-        in_specs=[pl.BlockSpec(memory_space=pltpu.VMEM)] * 4,
-        out_specs=(pl.BlockSpec(memory_space=pltpu.VMEM),) * 2,
-        scratch_shapes=[pltpu.VMEM((x.shape[0] + 16, width), jnp.bfloat16)],
+        in_specs=[pl.BlockSpec(memory_space=pltpu.VMEM)] * 3,
+        out_specs=(pl.BlockSpec(memory_space=pltpu.HBM), pl.BlockSpec(memory_space=pltpu.VMEM)),
+        scratch_shapes=[pltpu.SemaphoreType.DMA],
         compiler_params=pltpu.CompilerParams(vmem_limit_bytes=40 * 2**20),
         name="finish",
-    )(whitener, lagged_cov, average, x)
+    )(whitener, lagged_cov, whitened)
 
 
 def on_device(codes, row_scale, valid):

time: 63.2 us -> 65.2 us (1.032)
  Pallas kernels: 60.1 us -> 62 us
    pallas_call x2, Pallas kernels: 60.1 us -> 62 us  [the longest x1 58.7 us: moments(): pl.pallas_call(moments_kernel, out_shape=(square, square, jax.ShapeDtypeS...]
where the time goes in v4:
time: 65.2 us; the launch traced here: 65.1 us
  Pallas kernels  62 us (95%)
  local copies, waits for them, and re-layouts  1.62 us (2%)
  between operations  1.45 us (2%)
    pallas_call x1, Pallas kernels, moments(): pl.pallas_call(moments_kernel, out_shape=(square, square, jax.ShapeDtypeS...  58.7 us
    pallas_call x1, Pallas kernels, finish(): pl.pallas_call(finish_kernel, out_shape=(jax.ShapeDtypeStruct(whitened.sh...  3.26 us
    unnamed x4, local copies, waits for them, and re-layouts  1.62 us

profile of v4, /device:TPU:1, one launch (start us, length us, event | category | flops | bytes accessed | tf_op | source)
XLA Modules:
  0.0 65.1 jit_solution(15038205712169445074)
XLA Ops:
  1.3 0.0 copy-start.1
  1.3 0.7 %copy-done.1 = f32[1,256]{1,0:T(1,128)S(1)} copy-done((f32[1,256]{1,0:T(1,128)S(1)}, f32[1,256]{1,0:T(1,128)}, u32[]{:S(2)}) %copy-start.1) | copy-done | bytes 1048
  2.0 0.0 copy-start
  2.0 0.9 %copy-done = bf16[1,256,512]{2,1,0:T(8,128)(2,1)S(1)} copy-done((bf16[1,256,512]{2,1,0:T(8,128)(2,1)S(1)}, bf16[1,256,512]{2,1,0:T(8,128)(2,1)}, u32[]{:S(2)}) %copy-start) | copy-done | bytes 262168
  2.9 58.7 %moments.1 = (f32[512,512]{1,0:T(8,128)S(1)}, f32[512,512]{1,0:T(8,128)S(1)}, bf16[256,512]{1,0:T(8,128)(2,1)S(1)}) custom-call(bf16[256,512]{1,0:T(8,128)(2,1)S(1)} %bitcast.2, f32[1,256]{1,0:T(1,128)S(1)} %copy-done.1, s32[1]{0:T(128)S(6)} %copy.5.valid_ref), custom_call_target="tpu_custom_call" | custom-call | tf_op jit(solution)/shard_map/moments/pallas_call | solution.py:358
  61.6 3.3 %finish.1 = (bf16[256,512]{1,0:T(8,128)(2,1)}, f32[512,512]{1,0:T(8,128)}) custom-call(f32[512,512]{1,0:T(8,128)S(1)} %get-tuple-element.7.A, f32[512,512]{1,0:T(8,128)S(1)} %get-tuple-element.8.S, bf16[256,512]{1,0:T(8,128)(2,1)S(1)} %get-tuple-element.9.white_in), custom_call_target="tpu_custom_call" | custom-call | tf_op jit(solution)/shard_map/finish/pallas_call | solution.py:590
Async XLA Ops:
  1.3 0.7 %copy-start.1 = (f32[1,256]{1,0:T(1,128)S(1)}, f32[1,256]{1,0:T(1,128)}, u32[]{:S(2)}) copy-start(f32[1,256]{1,0:T(1,128)} %scale_in.1) | copy-start | bytes 3076
  2.0 0.9 %copy-start = (bf16[1,256,512]{2,1,0:T(8,128)(2,1)S(1)}, bf16[1,256,512]{2,1,0:T(8,128)(2,1)}, u32[]{:S(2)}) copy-start(bf16[1,256,512]{2,1,0:T(8,128)(2,1)} %param.3) | copy-start | bytes 786436

commit v5 on v3

--- a/solution.py
+++ b/solution.py
@@ -163,8 +163,8 @@
                 self.out[self.place.core, pl.ds(run.home, run.now_rows)] = run.now[...]
 
 
-def moments_kernel(
-    codes_in, scale_in, valid_ref, A, S, avg_ref, x_ref, codes_ref, scale_ref, load_sem, frames, turned, weighted, trailing, acc, summed, *rest
+def tica_kernel(
+    codes_in, scale_in, valid_ref, white_out, koop_out, A, S, white, koop, out_sem, codes_ref, scale_ref, load_sem, lhs, frames, turned, weighted, trailing, acc, summed, *rest
 ):
     (frame_send, frame_recv), rest = rest[:2], rest[2:]
     n = sum(kind != "ag" for part in PARTS for kind, _ in all_steps(part))
@@ -206,7 +206,7 @@
             codes = codes_ref[128 * i : 128 * i + 128, 128 * p : 128 * p + 128]
             x = (codes.astype(f32) * scale).astype(bf16)
             frames[p, at, :] = x
-            x_ref[128 * i : 128 * i + 128, 128 * p : 128 * p + 128] = x
+            lhs[128 * i : 128 * i + 128, 128 * p : 128 * p + 128] = x
 
     pl.semaphore_wait(barrier, len(greeted) - 1 + 2 * (1 - core))
     own = frames.at[:, pl.ds(mine, 256), :]
@@ -306,12 +306,25 @@
     eliminate(A, 3, D, lambda: lagged.advance(3))
     A[at_block(0), at_block(1)] = jnp.zeros((128, 128), f32)
     A[at_block(2), at_block(3)] = jnp.zeros((128, 128), f32)
-    avg_ref[...] = jnp.concatenate(means.avg + means.avg, axis=0)
+    whiten(A, means.avg, lhs, white)
+    out_white = pltpu.make_async_copy(white, white_out, out_sem.at[0])
+    out_white.start()
     lagged.arrive()
     means.lagged_cov(S)
+    out_koop = []
+
+    def written(i):
+        half = pl.ds(256 * i, 256)
+        out_koop.append(pltpu.make_async_copy(koop.at[half], koop_out.at[half], out_sem.at[1 + i]))
+        out_koop[-1].start()
+
+    whiten_lagged(A, S, koop, written)
     instant.close()
     lagged.close()
     swap.wait_send()
+    out_white.wait()
+    for c in out_koop:
+        c.wait()
 
     @pl.when(core == 0)
     def _():
@@ -343,20 +356,24 @@
     ]
 
 
-def moments(codes, row_scale, valid):
-    vmem = pl.BlockSpec(memory_space=pltpu.VMEM)
+def tica(codes, row_scale, valid):
     hbm = pl.BlockSpec(memory_space=pltpu.HBM)
     square = jax.ShapeDtypeStruct((codes.shape[1], codes.shape[1]), jnp.float32)
-    average = jax.ShapeDtypeStruct((8, 128), jnp.float32)
     return pl.pallas_call(
-        moments_kernel,
-        out_shape=(square, square, average, jax.ShapeDtypeStruct(codes.shape, codes.dtype)),
+        tica_kernel,
+        out_shape=(jax.ShapeDtypeStruct(codes.shape, codes.dtype), square),
         in_specs=[hbm, hbm, pl.BlockSpec(memory_space=pltpu.SMEM)],
-        out_specs=(vmem,) * 4,
+        out_specs=(hbm, hbm),
         scratch_shapes=[
+            pltpu.VMEM(square.shape, square.dtype),
+            pltpu.VMEM(square.shape, square.dtype),
+            pltpu.VMEM(codes.shape, codes.dtype),
+            pltpu.VMEM(square.shape, square.dtype),
+            pltpu.SemaphoreType.DMA((3,)),
             pltpu.VMEM(codes.shape, codes.dtype),
             pltpu.VMEM(row_scale.shape, row_scale.dtype),
             pltpu.SemaphoreType.DMA((2,)),
+            pltpu.VMEM((codes.shape[0] + 16, codes.shape[1]), jnp.bfloat16),
             pltpu.VMEM((4, 512 + LAG, 128), jnp.bfloat16),
             pltpu.VMEM((4, 4, 128, 128), jnp.bfloat16),
             pltpu.VMEM((4, 512, 128), jnp.bfloat16),
@@ -369,9 +386,9 @@
             *sum_scratch(),
         ],
         compiler_params=pltpu.CompilerParams(
-            collective_id=0, has_side_effects=True, vmem_limit_bytes=40 * 2**20
+            collective_id=0, has_side_effects=True, vmem_limit_bytes=58 * 2**20
         ),
-        name="moments",
+        name="tica",
     )(codes, row_scale, valid)
 
 
@@ -537,13 +554,8 @@
             )
 
 
-def finish_kernel(A, S, avg_ref, x_ref, white_ref, koop_ref, lhs):
-    f32 = jnp.float32
-    avg = [avg_ref[j : j + 1, :] for j in range(4)]
+def whiten(A, avg, lhs, white_ref):
     a = [A[0:256, 0:256], A[256:512, 0:256], A[256:512, 256:512]]
-    s = [S[0:256, 0:256], S[256:512, 0:256], S[256:512, 256:512]]
-    x = x_ref[...]
-    lhs[0:256, :] = x
     am = [jnp.concatenate([t[m] for t in [split3(q) for q in avg]], axis=1) for m in range(3)]
     lhs[256:272, :] = jnp.concatenate(am + [jnp.zeros((13, 512), jnp.bfloat16)], axis=0)
     y = [None, None]
@@ -556,6 +568,11 @@
     for h in range(2):
         m = y[h][256:257] + y[h][257:258] + y[h][258:259]
         white_ref[:, 256*h:256*h+256] = (y[h][0:256] - m).astype(jnp.bfloat16)
+
+
+def whiten_lagged(A, S, koop_ref, written):
+    a = [A[0:256, 0:256], A[256:512, 0:256], A[256:512, 256:512]]
+    s = [S[0:256, 0:256], S[256:512, 0:256], S[256:512, 256:512]]
     nn = ROWS; nt = LANES
     t00 = dot(a[0], s[0], nn)
     t10 = dot(a[1], s[0], nn) + dot(a[2], s[1], nn)
@@ -564,31 +581,17 @@
     k01 = dot(t00, a[1], nt)
     k10 = dot(t10, a[0], nt)
     k11 = dot(t10, a[1], nt) + dot(t11, a[2], nt)
+    k10 = k10 + jnp.transpose(k01)
     koop_ref[0:256, 0:256] = k00 + jnp.transpose(k00)
+    koop_ref[0:256, 256:512] = jnp.transpose(k10)
+    written(0)
+    koop_ref[256:512, 0:256] = k10
     koop_ref[256:512, 256:512] = k11 + jnp.transpose(k11)
-    k10 = k10 + jnp.transpose(k01)
-    koop_ref[256:512, 0:256] = k10
-    koop_ref[0:256, 256:512] = jnp.transpose(k10)
-
-
-def finish(whitener, lagged_cov, average, x):
-    width = x.shape[1]
-    return pl.pallas_call(
-        finish_kernel,
-        out_shape=(
-            jax.ShapeDtypeStruct(x.shape, jnp.bfloat16),
-            jax.ShapeDtypeStruct((width, width), jnp.float32),
-        ),
-        in_specs=[pl.BlockSpec(memory_space=pltpu.VMEM)] * 4,
-        out_specs=(pl.BlockSpec(memory_space=pltpu.VMEM),) * 2,
-        scratch_shapes=[pltpu.VMEM((x.shape[0] + 16, width), jnp.bfloat16)],
-        compiler_params=pltpu.CompilerParams(vmem_limit_bytes=40 * 2**20),
-        name="finish",
-    )(whitener, lagged_cov, average, x)
+    written(1)
 
 
 def on_device(codes, row_scale, valid):
-    projected, koopman = finish(*moments(codes[0], row_scale, valid))
+    projected, koopman = tica(codes[0], row_scale, valid)
     return (projected[None], koopman)
 
 

time: 63.2 us -> 64.8 us (1.025)
  local copies, waits for them, and re-layouts: 1.62 us -> 3.93 us
  Pallas kernels: 60.1 us -> 59.4 us
    unnamed x4 -> x2, local copies, waits for them, and re-layouts: 1.62 us -> 3.93 us
    pallas_call x2 -> x1, Pallas kernels: 60.1 us -> 59.4 us  [tica(): pl.pallas_call(tica_kernel, out_shape=(jax.ShapeDtypeStruct(codes.shape,...]
where the time goes in v5:
time: 64.8 us; the launch traced here: 64.6 us
  Pallas kernels  59.4 us (92%)
  local copies, waits for them, and re-layouts  3.93 us (6%)
  between operations  1.29 us (2%)
    pallas_call x1, Pallas kernels, tica(): pl.pallas_call(tica_kernel, out_shape=(jax.ShapeDtypeStruct(codes.shape,...  59.4 us
    unnamed x2, local copies, waits for them, and re-layouts  3.93 us

profile of v5, /device:TPU:1, one launch (start us, length us, event | category | flops | bytes accessed | tf_op | source)
XLA Modules:
  0.0 64.6 jit_solution(11548969644227911087)
XLA Ops:
  1.3 59.4 %tica.1 = (bf16[256,512]{1,0:T(8,128)(2,1)}, f32[512,512]{1,0:T(8,128)}) custom-call(bf16[256,512]{1,0:T(8,128)(2,1)} %bitcast.2, f32[1,256]{1,0:T(1,128)} %scale_in.1, s32[1]{0:T(128)S(6)} %copy.7.valid_ref), custom_call_target="tpu_custom_call" | custom-call | tf_op jit(solution)/shard_map/tica/pallas_call | solution.py:362
  60.7 1.7 %copy.8 = bf16[1,256,512]{2,1,0:T(8,128)(2,1)} copy(bf16[1,256,512]{2,1,0:T(8,128)(2,1)} %bitcast.3) | data formatting | bytes 524288
  62.3 2.3 %copy.9 = f32[512,512]{1,0:T(8,128)} copy(f32[512,512]{1,0:T(8,128)} %get-tuple-element.9) | data formatting | bytes 2097152

commit v6 on v5

--- a/solution.py
+++ b/solution.py
@@ -590,8 +590,32 @@
     written(1)
 
 
+def hand_on_kernel(white_in, koop_in, white_out, koop_out, sems):
+    copies = []
+    for source, target, pieces in ((koop_in, koop_out, 4), (white_in, white_out, 2)):
+        for i in range(pieces):
+            rows = pl.ds(128 * i, 128)
+            copies.append(pltpu.make_async_copy(source.at[rows], target.at[rows], sems.at[len(copies)]))
+            copies[-1].start()
+    for c in copies:
+        c.wait()
+
+
+def hand_on(whitened, koopman):
+    hbm = pl.BlockSpec(memory_space=pltpu.HBM)
+    return pl.pallas_call(
+        hand_on_kernel,
+        out_shape=tuple(jax.ShapeDtypeStruct(x.shape, x.dtype) for x in (whitened, koopman)),
+        in_specs=[hbm, hbm],
+        out_specs=(hbm, hbm),
+        scratch_shapes=[pltpu.SemaphoreType.DMA((6,))],
+        compiler_params=pltpu.CompilerParams(vmem_limit_bytes=58 * 2**20),
+        name="hand_on",
+    )(whitened, koopman)
+
+
 def on_device(codes, row_scale, valid):
-    projected, koopman = tica(codes[0], row_scale, valid)
+    projected, koopman = hand_on(*tica(codes[0], row_scale, valid))
     return (projected[None], koopman)
 
 

time: 64.8 us -> 102 us (1.57)
  Pallas kernels: 59.4 us -> 100 us
  local copies, waits for them, and re-layouts: 3.93 us -> 0 us
    pallas_call x0 -> x1, Pallas kernels: none -> 40.9 us  [hand_on(): pl.pallas_call(hand_on_kernel, out_shape=tuple((jax.ShapeDtypeStruct(x.sh...]
    unnamed x2 -> x0, local copies, waits for them, and re-layouts: 3.93 us -> none
where the time goes in v6:
time: 102 us
  Pallas kernels  100 us (98%)
  between operations  1.44 us (1%)
    pallas_call x1, Pallas kernels, tica(): pl.pallas_call(tica_kernel, out_shape=(jax.ShapeDtypeStruct(codes.shape,...  59.4 us
    pallas_call x1, Pallas kernels, hand_on(): pl.pallas_call(hand_on_kernel, out_shape=tuple((jax.ShapeDtypeStruct(x.sh...  40.9 us

profile of v6, /device:TPU:1, one launch (start us, length us, event | category | flops | bytes accessed | tf_op | source)
XLA Modules:
  0.0 101.7 jit_solution(12163894960623002087)
XLA Ops:
  1.3 59.4 %tica.1 = (bf16[256,512]{1,0:T(8,128)(2,1)}, f32[512,512]{1,0:T(8,128)}) custom-call(bf16[256,512]{1,0:T(8,128)(2,1)} %bitcast.2, f32[1,256]{1,0:T(1,128)} %scale_in.1, s32[1]{0:T(128)S(6)} %copy.5.valid_ref), custom_call_target="tpu_custom_call" | custom-call | tf_op jit(solution)/shard_map/tica/pallas_call | solution.py:362
  60.6 40.9 %hand_on.1 = (bf16[256,512]{1,0:T(8,128)(2,1)}, f32[512,512]{1,0:T(8,128)}) custom-call(bf16[256,512]{1,0:T(8,128)(2,1)} %get-tuple-element.6.white_in, f32[512,512]{1,0:T(8,128)} %get-tuple-element.7.koop_in), custom_call_target="tpu_custom_call" | custom-call | tf_op jit(solution)/shard_map/hand_on/pallas_call | solution.py:606

commit v7 on v6

--- a/solution.py
+++ b/solution.py
@@ -590,15 +590,19 @@
     written(1)
 
 
-def hand_on_kernel(white_in, koop_in, white_out, koop_out, sems):
-    copies = []
-    for source, target, pieces in ((koop_in, koop_out, 4), (white_in, white_out, 2)):
-        for i in range(pieces):
-            rows = pl.ds(128 * i, 128)
-            copies.append(pltpu.make_async_copy(source.at[rows], target.at[rows], sems.at[len(copies)]))
-            copies[-1].start()
-    for c in copies:
-        c.wait()
+def hand_on_kernel(white_in, koop_in, white_out, koop_out, white, koop, sems):
+    pieces = [(koop_in, koop, koop_out, i) for i in range(4)] + [(white_in, white, white_out, i) for i in range(2)]
+    loads, stores = [], []
+    for k, (source, held, target, i) in enumerate(pieces):
+        rows = pl.ds(128 * i, 128)
+        loads.append(pltpu.make_async_copy(source.at[rows], held.at[rows], sems.at[0, k]))
+        stores.append(pltpu.make_async_copy(held.at[rows], target.at[rows], sems.at[1, k]))
+        loads[-1].start()
+    for load, store in zip(loads, stores):
+        load.wait()
+        store.start()
+    for store in stores:
+        store.wait()
 
 
 def hand_on(whitened, koopman):
@@ -608,7 +612,11 @@
         out_shape=tuple(jax.ShapeDtypeStruct(x.shape, x.dtype) for x in (whitened, koopman)),
         in_specs=[hbm, hbm],
         out_specs=(hbm, hbm),
-        scratch_shapes=[pltpu.SemaphoreType.DMA((6,))],
+        scratch_shapes=[
+            pltpu.VMEM(whitened.shape, whitened.dtype),
+            pltpu.VMEM(koopman.shape, koopman.dtype),
+            pltpu.SemaphoreType.DMA((2, 6)),
+        ],
         compiler_params=pltpu.CompilerParams(vmem_limit_bytes=58 * 2**20),
         name="hand_on",
     )(whitened, koopman)

time: 102 us -> 63.1 us (0.62)
  Pallas kernels: 100 us -> 61.5 us
    pallas_call x1, Pallas kernels: 40.9 us -> 2.1 us  [hand_on(): pl.pallas_call(hand_on_kernel, out_shape=tuple((jax.ShapeDtypeStruct(x.sh...]
where the time goes in v7:
time: 63.1 us; the launch traced here: 62.9 us
  Pallas kernels  61.5 us (97%)
  between operations  1.44 us (2%)
    pallas_call x1, Pallas kernels, tica(): pl.pallas_call(tica_kernel, out_shape=(jax.ShapeDtypeStruct(codes.shape,...  59.4 us
    pallas_call x1, Pallas kernels, hand_on(): pl.pallas_call(hand_on_kernel, out_shape=tuple((jax.ShapeDtypeStruct(x.sh...  2.1 us

profile of v7, /device:TPU:1, one launch (start us, length us, event | category | flops | bytes accessed | tf_op | source)
XLA Modules:
  0.0 62.9 jit_solution(2613989426246916006)
XLA Ops:
  1.3 59.4 %tica.1 = (bf16[256,512]{1,0:T(8,128)(2,1)}, f32[512,512]{1,0:T(8,128)}) custom-call(bf16[256,512]{1,0:T(8,128)(2,1)} %bitcast.2, f32[1,256]{1,0:T(1,128)} %scale_in.1, s32[1]{0:T(128)S(6)} %copy.5.valid_ref), custom_call_target="tpu_custom_call" | custom-call | tf_op jit(solution)/shard_map/tica/pallas_call | solution.py:362
  60.6 2.1 %hand_on.1 = (bf16[256,512]{1,0:T(8,128)(2,1)}, f32[512,512]{1,0:T(8,128)}) custom-call(bf16[256,512]{1,0:T(8,128)(2,1)} %get-tuple-element.6.white_in, f32[512,512]{1,0:T(8,128)} %get-tuple-element.7.koop_in), custom_call_target="tpu_custom_call" | custom-call | tf_op jit(solution)/shard_map/hand_on/pallas_call | solution.py:610

commit v8 on v4

--- a/solution.py
+++ b/solution.py
@@ -7,11 +7,11 @@
 
 MESH = pl.DeviceIdType.MESH
 LAG = 64
-HALF = 576
+HALF = 544
 PARTS = (
-    (0, 128, "x", (("ar", "y"), ("ar", "z"))),
-    (128, 256, "y", (("ar", "z"), ("ar", "x"))),
-    (384, 192, "z", (("ar", "x"), ("ar", "y"))),
+    (0, 96, "x", (("ar", "y"), ("ar", "z"))),
+    (96, 192, "y", (("ar", "z"), ("ar", "x"))),
+    (288, 256, "z", (("ar", "x"), ("ar", "y"))),
 )
 SIZE = {"x": 4, "y": 8, "z": 8}
 FAR = {4: (2, 1, 3), 8: (4, 3, 5, 2, 6, 1, 7)}
@@ -78,7 +78,7 @@
         for run in self.runs[::-1]:
             self.begin(run, 0)
 
-    def advance(self, n, parts=(2, 0, 1)):
+    def advance(self, n, parts=(0, 1, 2)):
         for k in parts:
             run = self.runs[k]
             if n < len(run.steps):
@@ -295,20 +295,13 @@
     instant.advance(1)
     instant.advance(2)
     lagged.advance(0)
-    instant.advance(3, (2,))
-    instant.arrive((2,))
+    instant.advance(3)
+    lagged.advance(1)
+    instant.arrive()
     means = Means(summed.at[0], summed.at[1])
+    means.instant_cov(A)
     means.instant_diagonal(A)
-
-    def rest():
-        instant.advance(3, (0, 1))
-        lagged.advance(1)
-
-    def upper_blocks():
-        instant.arrive((0, 1))
-        means.instant_cov(A)
-
-    D = eliminate(A, 0, A[at_block(0), at_block(0)], rest, upper_blocks)
+    D = eliminate(A, 0, A[at_block(0), at_block(0)])
     D = eliminate(A, 1, D, lambda: lagged.advance(2))
     D = eliminate(A, 2, D)
     eliminate(A, 3, D, lambda: lagged.advance(3))
@@ -480,10 +473,8 @@
     return slice(128 * i, 128 * i + 128)
 
 
-def eliminate(A, k, D, halfway=None, others=None):
+def eliminate(A, k, D, halfway=None):
     W = jnp.concatenate(inverse_factor([D[8 * q : 8 * q + 8, :] for q in range(16)], halfway), axis=0)
-    if others is not None:
-        others()
     A[at_block(k), at_block(k)] = W
     if k < 3:
         near = dot(W, A[at_block(k), at_block(k + 1)], ROWS)

time: 65.2 us -> 63.4 us (0.972)
  Pallas kernels: 62 us -> 60.2 us
    pallas_call x1, Pallas kernels: 58.7 us -> 56.9 us  [moments(): pl.pallas_call(moments_kernel, out_shape=(square, square, jax.ShapeDtypeS...]
where the time goes in v8:
time: 63.4 us; the launch traced here: 63.3 us
  Pallas kernels  60.2 us (95%)
  local copies, waits for them, and re-layouts  1.62 us (3%)
  between operations  1.45 us (2%)
    pallas_call x1, Pallas kernels, moments(): pl.pallas_call(moments_kernel, out_shape=(square, square, jax.ShapeDtypeS...  56.9 us
    pallas_call x1, Pallas kernels, finish(): pl.pallas_call(finish_kernel, out_shape=(jax.ShapeDtypeStruct(whitened.sh...  3.26 us
    unnamed x4, local copies, waits for them, and re-layouts  1.62 us

profile of v8, /device:TPU:1, one launch (start us, length us, event | category | flops | bytes accessed | tf_op | source)
XLA Modules:
  0.0 63.3 jit_solution(18092703203835088229)
XLA Ops:
  1.3 0.0 copy-start.1
  1.3 0.7 %copy-done.1 = f32[1,256]{1,0:T(1,128)S(1)} copy-done((f32[1,256]{1,0:T(1,128)S(1)}, f32[1,256]{1,0:T(1,128)}, u32[]{:S(2)}) %copy-start.1) | copy-done | bytes 1048
  2.0 0.0 copy-start
  2.0 0.9 %copy-done = bf16[1,256,512]{2,1,0:T(8,128)(2,1)S(1)} copy-done((bf16[1,256,512]{2,1,0:T(8,128)(2,1)S(1)}, bf16[1,256,512]{2,1,0:T(8,128)(2,1)}, u32[]{:S(2)}) %copy-start) | copy-done | bytes 262168
  2.9 56.9 %moments.1 = (f32[512,512]{1,0:T(8,128)S(1)}, f32[512,512]{1,0:T(8,128)S(1)}, bf16[256,512]{1,0:T(8,128)(2,1)S(1)}) custom-call(bf16[256,512]{1,0:T(8,128)(2,1)S(1)} %bitcast.2, f32[1,256]{1,0:T(1,128)S(1)} %copy-done.1, s32[1]{0:T(128)S(6)} %copy.5.valid_ref), custom_call_target="tpu_custom_call" | custom-call | tf_op jit(solution)/shard_map/moments/pallas_call | solution.py:351
  59.8 3.3 %finish.1 = (bf16[256,512]{1,0:T(8,128)(2,1)}, f32[512,512]{1,0:T(8,128)}) custom-call(f32[512,512]{1,0:T(8,128)S(1)} %get-tuple-element.7.A, f32[512,512]{1,0:T(8,128)S(1)} %get-tuple-element.8.S, bf16[256,512]{1,0:T(8,128)(2,1)S(1)} %get-tuple-element.9.white_in), custom_call_target="tpu_custom_call" | custom-call | tf_op jit(solution)/shard_map/finish/pallas_call | solution.py:581
Async XLA Ops:
  1.3 0.7 %copy-start.1 = (f32[1,256]{1,0:T(1,128)S(1)}, f32[1,256]{1,0:T(1,128)}, u32[]{:S(2)}) copy-start(f32[1,256]{1,0:T(1,128)} %scale_in.1) | copy-start | bytes 3076
  2.0 0.9 %copy-start = (bf16[1,256,512]{2,1,0:T(8,128)(2,1)S(1)}, bf16[1,256,512]{2,1,0:T(8,128)(2,1)}, u32[]{:S(2)}) copy-start(bf16[1,256,512]{2,1,0:T(8,128)(2,1)} %param.3) | copy-start | bytes 786436
